TPU v7x, 32 devices: a whole 2x2x4 slice. The times are simulated.
32 devices in a mesh: dp: 32 (over z, y, x, core).
Axes of the slice: x: 2, y: 2, z: 4, core: 2. Of those that a mesh axis runs over, the one named last changes fastest.
Arguments:
- query_tokens: bfloat16 [1024, 768], P('dp'), may hold values from -6 to 6
- passage_tokens: bfloat16 [14080, 768], P('dp'), may hold values from -6 to 6
- query_lengths: int32 [32], P('dp'), may hold values from 5 to 32, as said below
- passage_lengths: int32 [64], P('dp'), may hold values from 28 to 220, as said below
- passage_valid: int32 [64], P('dp'), may hold values 0 or 1
- positives: int32 [32], P('dp'), may hold values from 0 to 63
- negatives: int32 [32], P('dp'), may hold values from 0 to 63
- teacher_margins: float32 [32], P('dp'), may hold values from -8 to 8
- query_grad: bfloat16 [1024, 768], P('dp'), may hold values from -6 to 6
- passage_grad: bfloat16 [14080, 768], P('dp'), may hold values from -6 to 6
- weight_query: bfloat16 [768, 768], replicated, may hold values from -0.21875 to 0.21875
- bias_query: bfloat16 [768], replicated, may hold values from -1.75 to 1.75
- weight_key: bfloat16 [768, 768], replicated, may hold values from -0.21875 to 0.21875
- weight_value: bfloat16 [768, 768], replicated, may hold values from -0.21875 to 0.21875
- bias_value: bfloat16 [768], replicated, may hold values from -0.625 to 0.625
- weight_out: bfloat16 [768, 768], replicated, may hold values from -1.25 to 1.25
- bias_out: bfloat16 [768], replicated, may hold values from -1.75 to 1.75
- gain_attn: bfloat16 [768], replicated, may hold values from 0.5 to 1.5
- shift_attn: bfloat16 [768], replicated, may hold values from -1.25 to 1.25
- weight_in: bfloat16 [768, 3072], replicated, may hold values from -0.21875 to 0.21875
- bias_in: bfloat16 [3072], replicated, may hold values from -1.75 to 1.75
- weight_back: bfloat16 [3072, 768], replicated, may hold values from -0.109375 to 0.109375
- bias_back: bfloat16 [768], replicated, may hold values from -1.75 to 1.75
- gain_ffn: bfloat16 [768], replicated, may hold values from 0.5 to 1.5
- shift_ffn: bfloat16 [768], replicated, may hold values from -1.25 to 1.25
Outputs:
- query_out: bfloat16 [1024, 768], P('dp')
- passage_out: bfloat16 [14080, 768], P('dp')
- query_loss: float32 [32], P('dp')
- query_tokens_grad: float32 [1024, 768], P('dp')
- passage_tokens_grad: float32 [14080, 768], P('dp')
- weight_query_grad: float32 [768, 768], P('dp')
- bias_query_grad: float32 [768], P('dp')
- weight_key_grad: float32 [768, 768], P('dp')
- weight_value_grad: float32 [768, 768], P('dp')
- bias_value_grad: float32 [768], P('dp')
- weight_out_grad: float32 [768, 768], P('dp')
- bias_out_grad: float32 [768], P('dp')
- gain_attn_grad: float32 [768], P('dp')
- shift_attn_grad: float32 [768], P('dp')
- weight_in_grad: float32 [768, 3072], P('dp')
- bias_in_grad: float32 [3072], P('dp')
- weight_back_grad: float32 [3072, 768], P('dp')
- bias_back_grad: float32 [768], P('dp')
- gain_ffn_grad: float32 [768], P('dp')
- shift_ffn_grad: float32 [768], P('dp')
Inputs may be any that keep to these rules, and one draw needn't show every extreme that they name: `query_lengths`: some query slot in every draw uses all 32 tokens. `passage_lengths`: some passage slot in every draw uses all 220 tokens.
All inputs are finite; a program needn't handle non-finite values. No bound on the sum of `passage_valid` on one device may be relied on, other than what follows from the above.
Results may differ from a plain program's by a relative error of at most 0.014.
Values may be sent and summed in bfloat16 or wider, within the bound.
A program may use at most 192 MiB of HBM per device.

v0:
```python
import jax
import jax.numpy as jnp
from jax import lax
from jax.experimental import pallas as pl
from jax.experimental.pallas import tpu as pltpu
from jax.sharding import PartitionSpec as P

D = 768
HEADS = 12
HEAD_DIM = 64


ln_eps = 1e-12
score_scale = 0.0625
margin_weight = 0.5
root_half = 0.7071067811865476
inv_root_tau = 0.3989422804014327


def matmul(left, right):
    return jnp.dot(left, right, preferred_element_type=jnp.float32)


def left_across(left, right):
    return lax.dot_general(
        left, right, (((0,), (0,)), ((), ())), preferred_element_type=jnp.float32
    )


def right_across(left, right):
    return lax.dot_general(
        left, right, (((1,), (1,)), ((), ())), preferred_element_type=jnp.float32
    )


def normalize(hidden, gain, shift):
    centered = hidden - jnp.mean(hidden, axis=-1, keepdims=True)
    inv_std = lax.rsqrt(jnp.mean(centered * centered, axis=-1, keepdims=True) + ln_eps)
    unit_rows = centered * inv_std
    return (unit_rows * gain.astype(jnp.float32) + shift.astype(jnp.float32), unit_rows, inv_std)


def normalize_back(upstream, unit_rows, inv_std, gain):
    scaled = upstream * gain.astype(jnp.float32)
    hidden_grad = inv_std * (
        scaled
        - jnp.mean(scaled, axis=-1, keepdims=True)
        - unit_rows * jnp.mean(scaled * unit_rows, axis=-1, keepdims=True)
    )
    return (hidden_grad, jnp.sum(upstream * unit_rows, axis=0), jnp.sum(upstream, axis=0))


def gelu_exact(inputs):
    return 0.5 * inputs * (1.0 + lax.erf(inputs * root_half))


def gelu_slope(inputs):
    return 0.5 * (1.0 + lax.erf(inputs * root_half)) + inputs * inv_root_tau * jnp.exp(
        -0.5 * inputs * inputs
    )


def head_scores(query_heads, key_heads, lengths):
    slot_length = query_heads.shape[1]
    allowed = (lax.iota(jnp.int32, slot_length)[None, :] < lengths[:, None])[:, None, None, :]
    raw_scores = 0.125 * jnp.einsum(
        "bqhd,bkhd->bhqk", query_heads, key_heads, preferred_element_type=jnp.float32
    )
    return jnp.where(allowed, raw_scores, -1000000000.0)


def encode_forward(tokens, lengths, params):
    (
        weight_query,
        bias_query,
        weight_key,
        weight_value,
        bias_value,
        weight_out,
        bias_out,
        gain_attn,
        shift_attn,
        weight_in,
        bias_in,
        weight_back,
        bias_back,
        gain_ffn,
        shift_ffn,
    ) = params
    slot_count = lengths.shape[0]
    row_count = tokens.shape[0]
    split_heads = (slot_count, row_count // slot_count, HEADS, HEAD_DIM)
    queries = (matmul(tokens, weight_query) + bias_query.astype(jnp.float32)).astype(jnp.bfloat16)
    keys_all = matmul(tokens, weight_key).astype(jnp.bfloat16)
    values_all = (matmul(tokens, weight_value) + bias_value.astype(jnp.float32)).astype(
        jnp.bfloat16
    )
    scores = head_scores(queries.reshape(split_heads), keys_all.reshape(split_heads), lengths)
    peak_score = jnp.max(scores, axis=-1, keepdims=True)
    exp_scores = jnp.exp(scores - peak_score)
    row_total = jnp.sum(exp_scores, axis=-1, keepdims=True)
    soft_low = (exp_scores / row_total).astype(jnp.bfloat16)
    log_total = peak_score + jnp.log(row_total)
    context = jnp.einsum(
        "bhqk,bkhd->bqhd",
        soft_low,
        values_all.reshape(split_heads),
        preferred_element_type=jnp.float32,
    )
    context = context.reshape(row_count, D).astype(jnp.bfloat16)
    attn_sum = (
        tokens.astype(jnp.float32) + matmul(context, weight_out) + bias_out.astype(jnp.float32)
    )
    middle, unit_attn, inv_attn = normalize(attn_sum, gain_attn, shift_attn)
    middle_low = middle.astype(jnp.bfloat16)
    inner_act = matmul(middle_low, weight_in) + bias_in.astype(jnp.float32)
    gelu_low = gelu_exact(inner_act).astype(jnp.bfloat16)
    ffn_sum = middle + matmul(gelu_low, weight_back) + bias_back.astype(jnp.float32)
    output, unit_ffn, inv_ffn = normalize(ffn_sum, gain_ffn, shift_ffn)
    kept = (
        queries,
        keys_all,
        values_all,
        log_total,
        context,
        unit_attn,
        inv_attn,
        middle_low,
        inner_act,
        gelu_low,
        unit_ffn,
        inv_ffn,
    )
    return (output.astype(jnp.bfloat16), kept)


def ffn_backward(upstream, kept, params):
    (
        queries,
        keys_all,
        values_all,
        log_total,
        context,
        unit_attn,
        inv_attn,
        middle_low,
        inner_act,
        gelu_low,
        unit_ffn,
        inv_ffn,
    ) = kept
    weight_in, weight_back, gain_ffn = (params[9], params[11], params[13])
    ffn_grad, gain_grad, shift_grad = normalize_back(upstream, unit_ffn, inv_ffn, gain_ffn)
    branch_low = ffn_grad.astype(jnp.bfloat16)
    back_weight_grad = left_across(gelu_low, branch_low)
    back_bias_grad = jnp.sum(branch_low, axis=0, dtype=jnp.float32)
    inner_low = (right_across(branch_low, weight_back) * gelu_slope(inner_act)).astype(jnp.bfloat16)
    in_weight_grad = left_across(middle_low, inner_low)
    in_bias_grad = jnp.sum(inner_low, axis=0, dtype=jnp.float32)
    middle_grad = ffn_grad + right_across(inner_low, weight_in)
    return (
        middle_grad,
        (in_weight_grad, in_bias_grad, back_weight_grad, back_bias_grad, gain_grad, shift_grad),
    )


def attention_backward(middle_grad, tokens, lengths, kept, params):
    (
        queries,
        keys_all,
        values_all,
        log_total,
        context,
        unit_attn,
        inv_attn,
        middle_low,
        inner_act,
        gelu_low,
        unit_ffn,
        inv_ffn,
    ) = kept
    weight_query, weight_key, weight_value, weight_out, gain_attn = (
        params[0],
        params[2],
        params[3],
        params[5],
        params[7],
    )
    slot_count = lengths.shape[0]
    row_count = tokens.shape[0]
    split_heads = (slot_count, row_count // slot_count, HEADS, HEAD_DIM)
    attn_grad, gain_grad, shift_grad = normalize_back(middle_grad, unit_attn, inv_attn, gain_attn)
    attn_low = attn_grad.astype(jnp.bfloat16)
    out_weight_grad = left_across(context, attn_low)
    out_bias_grad = jnp.sum(attn_low, axis=0, dtype=jnp.float32)
    context_grad = right_across(attn_low, weight_out).astype(jnp.bfloat16).reshape(split_heads)
    query_heads = queries.reshape(split_heads)
    key_heads = keys_all.reshape(split_heads)
    value_heads = values_all.reshape(split_heads)
    soft_full = jnp.exp(head_scores(query_heads, key_heads, lengths) - log_total)
    soft_grad = jnp.einsum(
        "bqhd,bkhd->bhqk", context_grad, value_heads, preferred_element_type=jnp.float32
    )
    value_grad = jnp.einsum(
        "bhqk,bqhd->bkhd",
        soft_full.astype(jnp.bfloat16),
        context_grad,
        preferred_element_type=jnp.float32,
    )
    value_grad = value_grad.reshape(row_count, D).astype(jnp.bfloat16)
    score_low = (
        soft_full * (soft_grad - jnp.sum(soft_full * soft_grad, axis=-1, keepdims=True))
    ).astype(jnp.bfloat16)
    query_grad_low = 0.125 * jnp.einsum(
        "bhqk,bkhd->bqhd", score_low, key_heads, preferred_element_type=jnp.float32
    )
    query_grad_low = query_grad_low.reshape(row_count, D).astype(jnp.bfloat16)
    key_grad_low = 0.125 * jnp.einsum(
        "bhqk,bqhd->bkhd", score_low, query_heads, preferred_element_type=jnp.float32
    )
    key_grad_low = key_grad_low.reshape(row_count, D).astype(jnp.bfloat16)
    token_grad = (
        attn_grad
        + right_across(query_grad_low, weight_query)
        + right_across(key_grad_low, weight_key)
        + right_across(value_grad, weight_value)
    )
    grads = (
        left_across(tokens, query_grad_low),
        jnp.sum(query_grad_low, axis=0, dtype=jnp.float32),
        left_across(tokens, key_grad_low),
        left_across(tokens, value_grad),
        jnp.sum(value_grad, axis=0, dtype=jnp.float32),
        out_weight_grad,
        out_bias_grad,
        gain_grad,
        shift_grad,
    )
    return (token_grad, grads)


def on_device(
    query_tokens,
    passage_tokens,
    query_lengths,
    passage_lengths,
    passage_valid,
    positives,
    negatives,
    teacher_margins,
    query_grad,
    passage_grad,
    weight_query,
    bias_query,
    weight_key,
    weight_value,
    bias_value,
    weight_out,
    bias_out,
    gain_attn,
    shift_attn,
    weight_in,
    bias_in,
    weight_back,
    bias_back,
    gain_ffn,
    shift_ffn,
):
    params = (
        weight_query,
        bias_query,
        weight_key,
        weight_value,
        bias_value,
        weight_out,
        bias_out,
        gain_attn,
        shift_attn,
        weight_in,
        bias_in,
        weight_back,
        bias_back,
        gain_ffn,
        shift_ffn,
    )
    query_out, query_kept = encode_forward(query_tokens, query_lengths, params)
    passage_out, passage_kept = encode_forward(passage_tokens, passage_lengths, params)
    query_slots = query_lengths.shape[0]
    passage_slots = passage_lengths.shape[0]
    cls_query = query_out.reshape(query_slots, -1, D)[:, 0]
    cls_passage = passage_out.reshape(passage_slots, -1, D)[:, 0]
    valid_low = passage_valid.astype(jnp.bfloat16)

    def score_piece(cls_piece, valid_piece):
        scores = score_scale * right_across(cls_query, cls_piece)
        position = lax.iota(jnp.int32, cls_piece.shape[0])
        is_positive = position[None, :] == positives[:, None]
        is_negative = position[None, :] == negatives[:, None]
        allowed = (valid_piece[None, :] > 0.5) | is_positive
        return (scores, allowed, is_positive, is_negative)

    peak_score = jnp.full((query_slots,), -1e30, jnp.float32)
    scores, allowed, is_positive, is_negative = score_piece(
        lax.all_gather(cls_passage, "dp", axis=0, tiled=True),
        lax.all_gather(valid_low, "dp", axis=0, tiled=True),
    )
    masked = jnp.where(allowed, scores, -1e30)
    new_peak = jnp.maximum(peak_score, jnp.max(masked, axis=1))
    row_total = jnp.sum(jnp.where(allowed, jnp.exp(masked - new_peak[:, None]), 0.0), axis=1)
    positive_score = jnp.sum(jnp.where(is_positive, scores, 0.0), axis=1)
    negative_score = jnp.sum(jnp.where(is_negative, scores, 0.0), axis=1)
    peak_score, row_total, positive_score, negative_score = (
        new_peak,
        row_total,
        positive_score,
        negative_score,
    )
    all_cls, all_valid = (
        lax.all_gather(cls_passage, "dp", axis=0, tiled=True),
        lax.all_gather(valid_low, "dp", axis=0, tiled=True),
    )
    log_total = peak_score + jnp.log(row_total)
    shortfall = positive_score - negative_score - teacher_margins
    query_loss = log_total - positive_score + margin_weight * shortfall * shortfall
    scores, allowed, is_positive, is_negative = score_piece(all_cls, all_valid)
    soft_scores = jnp.where(allowed, jnp.exp(scores - log_total[:, None]), 0.0)
    positive_hit = is_positive.astype(jnp.float32)
    negative_hit = is_negative.astype(jnp.float32)
    score_grad = (
        soft_scores
        - positive_hit
        + 2.0 * margin_weight * shortfall[:, None] * (positive_hit - negative_hit)
    ).astype(jnp.bfloat16)
    cls_query_grad = score_scale * matmul(score_grad, all_cls)
    cls_passage_grad = lax.psum_scatter(
        score_scale * left_across(score_grad, cls_query), "dp", scatter_dimension=0, tiled=True
    )
    query_upstream = (
        query_grad.astype(jnp.float32)
        .reshape(query_slots, -1, D)
        .at[:, 0]
        .add(cls_query_grad)
        .reshape(-1, D)
    )
    passage_upstream = (
        passage_grad.astype(jnp.float32)
        .reshape(passage_slots, -1, D)
        .at[:, 0]
        .add(cls_passage_grad)
        .reshape(-1, D)
    )
    query_middle_grad, query_ffn = ffn_backward(query_upstream, query_kept, params)
    passage_middle_grad, passage_ffn = ffn_backward(passage_upstream, passage_kept, params)
    (
        in_weight_grad,
        in_bias_grad,
        back_weight_grad,
        back_bias_grad,
        ffn_gain_grad,
        ffn_shift_grad,
    ) = tuple((first + second for first, second in zip(query_ffn, passage_ffn)))
    query_tokens_grad, query_attn = attention_backward(
        query_middle_grad, query_tokens, query_lengths, query_kept, params
    )
    passage_tokens_grad, passage_attn = attention_backward(
        passage_middle_grad, passage_tokens, passage_lengths, passage_kept, params
    )
    (
        query_weight_grad,
        query_bias_grad,
        key_weight_grad,
        value_weight_grad,
        value_bias_grad,
        out_weight_grad,
        out_bias_grad,
        attn_gain_grad,
        attn_shift_grad,
    ) = tuple((first + second for first, second in zip(query_attn, passage_attn)))
    (
        query_weight_grad,
        query_bias_grad,
        key_weight_grad,
        value_weight_grad,
        value_bias_grad,
        out_weight_grad,
        out_bias_grad,
        attn_gain_grad,
        attn_shift_grad,
        in_weight_grad,
        in_bias_grad,
        back_weight_grad,
        back_bias_grad,
        ffn_gain_grad,
        ffn_shift_grad,
    ) = (
        lax.psum_scatter(query_weight_grad, "dp", scatter_dimension=0, tiled=True),
        lax.psum_scatter(query_bias_grad, "dp", scatter_dimension=0, tiled=True),
        lax.psum_scatter(key_weight_grad, "dp", scatter_dimension=0, tiled=True),
        lax.psum_scatter(value_weight_grad, "dp", scatter_dimension=0, tiled=True),
        lax.psum_scatter(value_bias_grad, "dp", scatter_dimension=0, tiled=True),
        lax.psum_scatter(out_weight_grad, "dp", scatter_dimension=0, tiled=True),
        lax.psum_scatter(out_bias_grad, "dp", scatter_dimension=0, tiled=True),
        lax.psum_scatter(attn_gain_grad, "dp", scatter_dimension=0, tiled=True),
        lax.psum_scatter(attn_shift_grad, "dp", scatter_dimension=0, tiled=True),
        lax.psum_scatter(in_weight_grad, "dp", scatter_dimension=0, tiled=True),
        lax.psum_scatter(in_bias_grad, "dp", scatter_dimension=0, tiled=True),
        lax.psum_scatter(back_weight_grad, "dp", scatter_dimension=0, tiled=True),
        lax.psum_scatter(back_bias_grad, "dp", scatter_dimension=0, tiled=True),
        lax.psum_scatter(ffn_gain_grad, "dp", scatter_dimension=0, tiled=True),
        lax.psum_scatter(ffn_shift_grad, "dp", scatter_dimension=0, tiled=True),
    )
    return (
        query_out,
        passage_out,
        query_loss,
        query_tokens_grad,
        passage_tokens_grad,
        query_weight_grad,
        query_bias_grad,
        key_weight_grad,
        value_weight_grad,
        value_bias_grad,
        out_weight_grad,
        out_bias_grad,
        attn_gain_grad,
        attn_shift_grad,
        in_weight_grad,
        in_bias_grad,
        back_weight_grad,
        back_bias_grad,
        ffn_gain_grad,
        ffn_shift_grad,
    )


F32 = jnp.float32
BF16 = jnp.bfloat16
MESH = pl.DeviceIdType.MESH
FF = 3072
ROWS = 480
WIN = 240
SLOT = 220
NEG = -1000000000.0


def dot_nn(left, right):
    return jnp.dot(left, right, preferred_element_type=F32)


def dot_nt(left, right):
    return lax.dot_general(left, right, (((1,), (1,)), ((), ())), preferred_element_type=F32)


def dot_tn(left, right):
    return lax.dot_general(left, right, (((0,), (0,)), ((), ())), preferred_element_type=F32)


def row_of(ref, start=0, size=D):
    return ref[pl.ds(start, size)].astype(F32).reshape(1, size)


def one(ref):
    return ref[...].reshape(1, 1)


def blocks(start, stop, size):
    return [(at, min(size, stop - at)) for at in range(start, stop, size)]


def iota(shape, dim):
    return lax.broadcasted_iota(jnp.int32, shape, dim)


def fold8(block):
    return jnp.sum(block.reshape(-1, 8, block.shape[-1]), axis=0)


WIDE = 256
ROUTE = (
    "xyz", "yxz", "zyx", "xyz", "zxy", "zyx", "yxz", "xyz", "yxz", "xyz", "yxz", "xyz", "yxz", "xyz", "yxz", "xyz",
    "yxz", "xyz",
)
ORDER = (
    ("wback", 0, 0), ("c", 0, 0), ("wback", 0, 1), ("c", 0, 1), ("wback", 0, 2), ("c", 0, 2), ("wback", 1, 0),
    ("c", 1, 0), ("wback", 1, 1), ("c", 1, 1), ("wback", 1, 2), ("c", 1, 2), ("dinner", 0), ("ec", 0, 0),
    ("dinner", 1), ("ec", 0, 2), ("win", 2, 0), ("ec", 0, 1), ("c", 2, 0), ("win", 2, 1), ("ec", 1, 0), ("c", 2, 1),
    ("win", 2, 2), ("ec", 1, 2), ("ec", 1, 1), ("c", 2, 2), ("dinner", 2), ("dinner", 3), ("win", 3, 0), ("c", 3, 0),
    ("ec", 2, 0), ("win", 3, 1), ("ec", 2, 1), ("c", 3, 1), ("win", 3, 2), ("c", 3, 2), ("dmid", 0), ("dmid", 1),
    ("ec", 2, 2), ("dmid", 2), ("dmid", 3), ("lnback",), ("dctx",), ("ec", 3, 1), ("ec", 3, 0), ("qslot",),
    ("e1", 1, 0), ("attn", 0, 1), ("ec", 3, 2), ("attn", 1, 4), ("e1", 0, 2), ("e1", 2, 2), ("attn", 5, 1),
    ("sums",), ("wvo", 0), ("c", 4, 0), ("e1", 0, 1), ("e1", 2, 0), ("e1", 0, 0), ("wvo", 1), ("c", 4, 1),
    ("wvo", 2), ("e1", 3, 1), ("c", 4, 2), ("vec", 0), ("e1", 2, 1), ("ec", 4, 0), ("wqk", 0), ("c", 5, 0),
    ("ec", 4, 1), ("e2", 2, 2), ("e1", 3, 0), ("ec", 4, 2), ("e2", 0, 0), ("wqk", 1), ("e1", 3, 2), ("e2", 0, 1),
    ("c", 5, 1), ("e2", 1, 0), ("vec", 1), ("wqk", 2), ("c", 5, 2), ("e2", 3, 1), ("e1", 4, 0), ("e2", 2, 1),
    ("ec", 5, 2), ("e1", 4, 1), ("ec", 5, 1), ("e2", 2, 0), ("e3", 2, 2), ("e1", 4, 2), ("e2", 3, 0), ("ec", 5, 0),
    ("e3", 0, 1), ("e2", 4, 0), ("e1", 5, 2), ("tq",), ("e3", 2, 1), ("e2", 3, 2), ("e3", 2, 0), ("e2", 4, 2),
    ("e3", 3, 1), ("e1", 1, 2), ("e1", 1, 1), ("e2", 4, 1), ("e1", 5, 1), ("vec", 2), ("e1", 5, 0), ("e2", 5, 2),
    ("e3", 3, 2), ("e3", 1, 0), ("vec", 3), ("e2", 5, 1), ("e3", 0, 0), ("tk",), ("e3", 4, 0), ("e2", 0, 2),
    ("e2", 5, 0), ("e3", 4, 1), ("e2", 1, 1), ("e3", 4, 2), ("e2", 1, 2), ("e3", 1, 2), ("e3", 5, 1), ("e3", 3, 0),
    ("vecend",), ("tv",), ("tout",), ("e3", 5, 2), ("e3", 1, 1), ("e3", 0, 2), ("e3", 5, 0),
)


def layer_kernel(
    qtok, ptok, qlen_h, plen, pvalid, pos_h, neg_h, margin_h, qgrad, pgrad,
    wq_h, bq_h, wk_h, wv_h, bv_h, wo_h, bo_h, ga_h, sa_h, wi_h, bi_h, wb_h, bb_h, gf_h, sf_h,
    qout_h, pout_h, qtg_h, ptg_h, wqg, wkg, wvg, wog, wig, wbg, small_h,
    qlen, pos, neg, margin, bq, bv, bo, ga, sa, bi, bb, gf, sf, wq, wk, wv, wo, wi, wb, pstage, x_s, xT, q_s, k_s, v_s, p_s, pq_s, c_s, cT, n1, n2, r1, r2,
    ml, mlT, act_a, act_b, actT, tmp_a, tmp_b, gp, qg_s, pg_s, qo_s, po_s, ex, ex_f, vec, vecr, vecs, vecz, small_o, parts,
    g_s, rc, ra, rb, rz, rw,
    load_sem, out_sem, part_sem, ex_send, ex_recv, c_send, c_recv, a_send, a_recv, b_send, b_recv,
    z_send, z_recv, v_send, v_recv, credit,
):
    me = lax.axis_index("dp")
    core = lax.rem(me, 2)
    xx = lax.rem(lax.div(me, 2), 2)
    yy = lax.rem(lax.div(me, 4), 2)
    zz = lax.div(me, 8)
    chip = lax.div(me, 2)
    partner = me + 1 - 2 * core
    x_peer = me + 2 - 4 * xx
    y_peer = me + 4 - 8 * yy
    plane = lax.rem(me, 8)

    loads = {}

    def load(name, source, target):
        loads[name] = pltpu.make_async_copy(source, target, load_sem.at[len(loads)])
        loads[name].start()

    load("ptok", ptok, pstage)
    load("qtok", qtok, qo_s)
    load("wq", wq_h, wq)
    load("wk", wk_h, wk)
    load("wv", wv_h, wv)
    vectors = ((qlen_h, qlen), (pos_h, pos), (neg_h, neg), (margin_h, margin), (bq_h, bq), (bv_h, bv), (bo_h, bo), (ga_h, ga), (sa_h, sa), (bi_h, bi), (bb_h, bb), (gf_h, gf), (sf_h, sf))
    for at, (source, target) in enumerate(vectors):
        load("vec" + str(at), source, target)

    barrier = pltpu.get_barrier_semaphore()
    for hop in range(1, 16):
        other = 2 * lax.rem(chip + hop, 16) + core
        pl.semaphore_signal(barrier, inc=1, device_id=(other,), device_id_type=MESH)
    pl.semaphore_signal(barrier, inc=1, device_id=(partner,), device_id_type=MESH)

    loads["ptok"].wait()
    loads["qtok"].wait()
    x_s[0:32, :] = qo_s[...]

    def copy_tokens(i, carry):
        x_s[pl.ds(pl.multiple_of(32 + i * 16, 16), 16), :] = pstage[pl.ds(pl.multiple_of(i * 16, 16), 16), :]
        return carry

    lax.fori_loop(0, 27, copy_tokens, 0)
    x_s[464:480, :] = jnp.concatenate(
        [pstage[432:440, :].astype(F32), jnp.zeros((8, D), F32)], axis=0
    ).astype(BF16)

    loads["wq"].wait()
    for at in range(len(vectors)):
        loads["vec" + str(at)].wait()
    load("wo", wo_h, wo)
    load("wi", wi_h, wi)
    q_s[...] = ((dot_nn(x_s[...], wq[...]) + row_of(bq)).astype(BF16) * 0.125).astype(BF16)
    loads["wk"].wait()
    k_s[...] = dot_nn(x_s[...], wk[...]).astype(BF16)
    loads["wv"].wait()
    for h in range(3):
        load("wb" + str(h), wb_h.at[:, :, :, :, :, :, pl.ds(WIDE * h, WIDE)], wb.at[h])
    load("qg", qgrad, qg_s)
    load("pg", pgrad, pg_s)
    v_s[...] = (dot_nn(x_s[...], wv[...]) + row_of(bv)).astype(BF16)

    head_of = iota((12, 1, D), 2) // 64
    head_mask = (head_of == iota((12, 1, D), 0)).astype(F32)

    def spread(rows):
        return (rows.astype(F32)[None] * head_mask).astype(BF16).reshape(384, D)

    def gather_heads(stacked):
        return jnp.sum(stacked.reshape(12, 32, D) * head_mask, axis=0)

    raw = dot_nt(k_s[0:32, :], spread(q_s[0:32, :]))
    raw = jnp.where(iota((32, 384), 0) < one(qlen), raw, NEG)
    soft = jnp.exp(raw - jnp.max(raw, axis=0, keepdims=True))
    soft = (soft * (1.0 / jnp.sum(soft, axis=0, keepdims=True))).astype(BF16)
    pq_s[...] = soft
    c_s[0:32, :] = gather_heads(dot_tn(soft, v_s[0:32, :])).astype(BF16)

    lane = iota((1, 128), 1)
    half = ((lane < 64).astype(BF16), (lane >= 64).astype(BF16))
    key_at = iota((WIN, 1), 0)

    def attend(pair, slot):
        lanes = pl.ds(pl.multiple_of(pair * 128, 128), 128)
        low_at = 12 * slot
        first_row = 32 + 208 * slot
        rows = pl.ds(first_row, WIN)
        keys, queries = k_s[rows, lanes], q_s[rows, lanes]
        values_t = v_s[rows, lanes].T
        allowed = (key_at >= low_at) & (key_at < low_at + plen[slot])
        parts = []
        for h in range(2):
            scores = jnp.where(allowed, dot_nt(keys, queries * half[h]), NEG)
            e = jnp.exp(scores - jnp.max(scores, axis=0, keepdims=True))
            p = (e * (1.0 / jnp.sum(e, axis=0, keepdims=True))).astype(BF16)
            p_s[slot, 2 * pair + h] = p
            parts.append(dot_nn(values_t, p)[64 * h:64 * h + 64, :])
        context = jnp.concatenate(parts, axis=0).T
        if slot == 0:
            c_s[rows, lanes] = context.astype(BF16)
            return
        old = c_s[240:256, lanes].astype(F32)
        c_s[240:256, lanes] = jnp.where(iota((16, 128), 0) >= 12, context[0:16], old).astype(BF16)
        c_s[256:480, lanes] = context[16:240].astype(BF16)

    def both_slots(pair, carry):
        attend(pair, 0)
        attend(pair, 1)
        return carry

    lax.fori_loop(0, 6, both_slots, 0)

    loads["wo"].wait()
    gain1, shift1, bias1 = row_of(ga), row_of(sa), row_of(bo)
    gain2, shift2, bias2 = row_of(gf), row_of(sf), row_of(bb)

    def wb_tile(t):
        return jnp.concatenate([wb[h, t // 2, t % 2].reshape(D, WIDE) for h in range(3)], axis=1)

    def normalized(hidden):
        centered = hidden - jnp.mean(hidden, axis=-1, keepdims=True)
        inv = lax.rsqrt(jnp.mean(centered * centered, axis=-1, keepdims=True) + ln_eps)
        return centered * inv, inv

    def forward_rows(start, stop):
        size = stop - start
        every, own = pl.ds(start, size), pl.ds(0, size)
        tmp_a[own, :] = dot_nn(c_s[every, :], wo[...])
        for at, count in blocks(0, size, 32):
            rows, here = pl.ds(start + at, count), pl.ds(at, count)
            unit, inv = normalized(tmp_a[here, :] + x_s[rows, :].astype(F32) + bias1)
            n1[rows, :] = unit
            r1[rows, :] = inv
            ml[rows, :] = (unit * gain1 + shift1).astype(BF16)
        if start == 0:
            loads["wi"].wait()
            for h in range(3):
                loads["wb" + str(h)].wait()
        inner, acts = (tmp_a, tmp_b), (act_a, act_b)
        tmp_a[own, :] = dot_nn(ml[every, :], wi[:, 0:D])
        mlT[:, every] = ml[every, :].T
        xT[:, every] = x_s[every, :].T
        cT[:, every] = c_s[every, :].T

        def finish(t):
            act = acts[t % 2][own, :]
            if t == 0:
                n2[every, :] = dot_nn(act, wb_tile(t))
            else:
                n2[every, :] += dot_nn(act, wb_tile(t))
            actT[t * D:t * D + D, every] = act.T

        for t in range(4):
            if t < 3:
                inner[(t + 1) % 2][own, :] = dot_nn(ml[every, :], wi[:, t * D + D:t * D + 2 * D])
            bias_t = row_of(bi, t * D)
            for at, count in blocks(0, size, 16):
                here = pl.ds(at, count)
                u = inner[t % 2][here, :] + bias_t
                cdf = 0.5 * (1.0 + lax.erf(u * root_half))
                acts[t % 2][here, :] = (u * cdf).astype(BF16)
                gp[start + at:start + at + count, t * D:t * D + D] = (
                    cdf + u * inv_root_tau * jnp.exp(-0.5 * u * u)
                ).astype(BF16)
            if t > 0:
                finish(t - 1)
        finish(3)
        for at, count in blocks(start, stop, 32):
            rows = pl.ds(at, count)
            unit, inv = normalized(n2[rows, :] + (n1[rows, :] * gain1 + shift1) + bias2)
            n2[rows, :] = unit
            r2[rows, :] = inv
            out = (unit * gain2 + shift2).astype(BF16)
            if at == 0:
                qo_s[...] = out
            else:
                po_s[at - 32:min(at, 440), :] = out[0:min(count, 472 - at)]

    forward_rows(0, 256)

    slot_me = core * 16 + chip
    base = pl.multiple_of(slot_me * 32, 32)
    first_rows = (
        qo_s[0:16, :].astype(F32)[0:1],
        po_s[0:16, :].astype(F32)[0:1],
        po_s[208:224, :].astype(F32)[12:13],
    )
    lane_row = iota((1, 128), 1)
    meta = jnp.zeros((1, 128), F32)
    margin_0 = jnp.zeros((1, 128), F32) + one(margin)
    margin_1 = margin_0.astype(BF16).astype(F32)
    margin_2 = (margin_0 - margin_1).astype(BF16).astype(F32)
    for at, value in enumerate((
        pvalid[0].astype(F32), pvalid[1].astype(F32), one(pos).astype(F32), one(neg).astype(F32),
        margin_1, margin_2, margin_0 - margin_1 - margin_2,
    )):
        meta = jnp.where(lane_row == at, value, meta)
    pieces = [row[:, 128 * i:128 * i + 128] for row in first_rows for i in range(6)]
    ex[pl.ds(base, 32), :] = jnp.concatenate(pieces + [meta, jnp.zeros((13, 128), F32)], axis=0).astype(BF16)

    pl.semaphore_wait(barrier, 16)
    sends = []
    for hop in range(1, 16):
        block = ex.at[pl.ds(base, 32), :]
        sends.append(pltpu.make_async_remote_copy(
            src_ref=block, dst_ref=block, send_sem=ex_send.at[hop], recv_sem=ex_recv.at[hop],
            device_id=(2 * lax.rem(chip + hop, 16) + core,), device_id_type=MESH,
        ))
        sends[-1].start()

    forward_rows(256, 480)
    out_q = pltpu.make_async_copy(qo_s, qout_h, out_sem.at[0])
    out_p = pltpu.make_async_copy(po_s, pout_h, out_sem.at[1])
    out_q.start()
    out_p.start()
    loads["qg"].wait()
    loads["pg"].wait()

    def ffn_norm_back(r0, upstream, sums):
        rows = pl.ds(r0, upstream.shape[0])
        unit = n2[rows, :]
        scaled = upstream * gain2
        hidden_grad = r2[rows, :] * (
            scaled
            - jnp.mean(scaled, axis=-1, keepdims=True)
            - unit * jnp.mean(scaled * unit, axis=-1, keepdims=True)
        )
        n2[rows, :] = hidden_grad
        rounded = hidden_grad.astype(BF16)
        ml[rows, :] = rounded
        return (
            sums[0] + fold8(upstream * unit), sums[1] + fold8(upstream), sums[2] + fold8(rounded.astype(F32)),
        )

    zero8 = jnp.zeros((8, D), F32)
    sums = (zero8, zero8, zero8)

    def middle_block(i, sums):
        upstream = pg_s[pl.ds(pl.multiple_of(i * 32, 32), 32), :].astype(F32)
        return ffn_norm_back(pl.multiple_of(32 + i * 32, 32), upstream, sums)

    sums = lax.fori_loop(1, 6, middle_block, sums)
    sums = lax.fori_loop(7, 13, middle_block, sums)
    last = jnp.concatenate([pg_s[416:440, :].astype(F32), jnp.zeros((8, D), F32)], axis=0)
    sums = ffn_norm_back(448, last, sums)

    for send in sends:
        send.wait()
    same_core = ex.at[pl.ds(pl.multiple_of(core * 512, 512), 512), :]
    across = pltpu.make_async_remote_copy(
        src_ref=same_core, dst_ref=same_core, send_sem=ex_send.at[0], recv_sem=ex_recv.at[0],
        device_id=(partner,), device_id_type=MESH,
    )
    across.start()
    across.wait()

    ex_f[...] = ex[...].astype(F32)

    def first(r):
        return ex_f[pl.ds(r, 32, stride=32), :]

    cls_q = jnp.concatenate([first(i) for i in range(6)], axis=1)
    cls_0 = jnp.concatenate([first(6 + i) for i in range(6)], axis=1).astype(BF16)
    cls_1 = jnp.concatenate([first(12 + i) for i in range(6)], axis=1).astype(BF16)
    metas = first(18)
    metas_t = metas.T
    s0 = score_scale * dot_nt(cls_q.astype(BF16), cls_0)
    s1 = score_scale * dot_nt(cls_q.astype(BF16), cls_1)
    col = iota((1, 32), 1)
    passage = (4 * lax.rem(col, 16) + 2 * lax.div(col, 16)).astype(F32)
    at_pos, at_neg, wanted = metas[:, 2:3], metas[:, 3:4], metas[:, 4:5] + metas[:, 5:6] + metas[:, 6:7]
    pos0, pos1 = at_pos == passage, at_pos == passage + 1.0
    neg0, neg1 = at_neg == passage, at_neg == passage + 1.0
    m0 = jnp.where((metas_t[0:1, :] > 0.5) | pos0, s0, -1e30)
    m1 = jnp.where((metas_t[1:2, :] > 0.5) | pos1, s1, -1e30)
    peak = jnp.maximum(jnp.max(m0, axis=1, keepdims=True), jnp.max(m1, axis=1, keepdims=True))
    total = jnp.sum(jnp.exp(m0 - peak), axis=1, keepdims=True) + jnp.sum(jnp.exp(m1 - peak), axis=1, keepdims=True)
    lse = peak + jnp.log(total)

    def picked(where0, where1):
        return jnp.sum(jnp.where(where0, s0, 0.0), axis=1, keepdims=True) + jnp.sum(
            jnp.where(where1, s1, 0.0), axis=1, keepdims=True
        )

    at_positive = picked(pos0, pos1)
    miss = at_positive - picked(neg0, neg1) - wanted
    losses = lse - at_positive + margin_weight * miss * miss
    pos0, pos1, neg0, neg1 = (hit.astype(F32) for hit in (pos0, pos1, neg0, neg1))
    ds0 = (jnp.exp(m0 - lse) - pos0 + 2.0 * margin_weight * miss * (pos0 - neg0)).astype(BF16)
    ds1 = (jnp.exp(m1 - lse) - pos1 + 2.0 * margin_weight * miss * (pos1 - neg1)).astype(BF16)
    mine = iota((32, 1), 0) == slot_me
    mine_col = iota((1, 32), 1) == slot_me
    small_o[9:10, :] = jnp.sum(jnp.where(mine, losses, 0.0), axis=0, keepdims=True) + jnp.zeros((1, 128), F32)
    dq_all = score_scale * (dot_nn(ds0, cls_0) + dot_nn(ds1, cls_1))
    d_query = jnp.sum(jnp.where(mine, dq_all, 0.0), axis=0, keepdims=True)

    def passage_grad_row(ds):
        column = jnp.sum(jnp.where(mine_col, ds.astype(F32), 0.0), axis=1, keepdims=True)
        return score_scale * jnp.sum(column * cls_q, axis=0, keepdims=True)

    d_first = (d_query, passage_grad_row(ds0), passage_grad_row(ds1))

    row32 = iota((32, 1), 0)
    for r0, at, source, add in (
        (0, 0, qg_s[...], d_first[0]), (32, 0, pg_s[0:32, :], d_first[1]), (224, 28, pg_s[192:224, :], d_first[2]),
    ):
        upstream = source.astype(F32) + jnp.where(row32 == at, add, 0.0)
        sums = ffn_norm_back(r0, upstream, sums)
    vec[...] = jnp.zeros_like(vec)
    vec[5:6, :] = jnp.sum(sums[2], axis=0, keepdims=True)
    vec[6:7, :] = jnp.sum(sums[0], axis=0, keepdims=True)
    vec[7:8, :] = jnp.sum(sums[1], axis=0, keepdims=True)

    def chunk(p, h):
        return g_s.at[p, h] if p < 4 else wb.at[h, p - 4]

    z_slot = {}
    for at, way in enumerate(ROUTE):
        if way[0] == "z":
            z_slot[(at // 3, at % 3)] = len(z_slot)

    def route(p, h):
        return ROUTE[3 * p + h]

    def remote(source, target, send, recv, device):
        return pltpu.make_async_remote_copy(
            src_ref=source, dst_ref=target, send_sem=send, recv_sem=recv, device_id=(device,), device_id_type=MESH,
        )

    def step_c(p, h):
        return [remote(chunk(p, h).at[1 - core], rc.at[p % 2, h], c_send.at[p, h], c_recv.at[p, h], partner)]

    def along_z(p, h, pick, target):
        steps = []
        for hop in range(1, 4):
            to = lax.rem(zz + hop, 4)
            steps.append(remote(
                pick(to), target(hop - 1), z_send.at[p, h, hop - 1], z_recv.at[p, h, hop - 1], to * 8 + plane,
            ))
        return steps

    def step_1(p, h):
        mine, way = chunk(p, h), route(p, h)
        if way[0] == "z":
            return along_z(p, h, lambda to: mine.at[core, to], lambda i: rw.at[z_slot[(p, h)], i])
        away = mine.at[core, :, :, 1 - xx] if way == "xyz" else mine.at[core, :, 1 - yy]
        return [remote(away, ra.at[p, h], a_send.at[p, h], a_recv.at[p, h], x_peer if way == "xyz" else y_peer)]

    def step_2(p, h):
        mine, way = chunk(p, h), route(p, h)
        if way == "zyx":
            away, target = mine.at[core, zz, 1 - yy], rb.at[p, h, 0:2]
        elif way == "zxy":
            away, target = mine.at[core, zz, :, 1 - xx], rb.at[p, h, 0:2]
        elif way == "xyz":
            away, target = mine.at[core, :, 1 - yy, xx], rb.at[p, h]
        else:
            away, target = mine.at[core, :, yy, 1 - xx], rb.at[p, h]
        return [remote(away, target, b_send.at[p, h], b_recv.at[p, h], x_peer if way[1] == "x" else y_peer)]

    def step_3(p, h):
        mine = chunk(p, h)
        way = route(p, h)
        if way[0] == "z":
            away = mine.at[core, zz, yy, 1 - xx] if way == "zyx" else mine.at[core, zz, 1 - yy, xx]
            return [remote(
                away, rz.at[p, h, 0], a_send.at[p, h], a_recv.at[p, h], x_peer if way == "zyx" else y_peer,
            )]
        return along_z(p, h, lambda to: mine.at[core, to, yy, xx], lambda i: rz.at[p, h, i])

    def begin(steps):
        for step in steps:
            step.start()

    def finish_steps(steps):
        for step in steps:
            step.wait()

    def start_c(p, h):
        if p >= 2:
            pl.semaphore_wait(credit.at[p % 2, h], 1)
        begin(step_c(p, h))

    def end_c(p, h):
        finish_steps(step_c(p, h))

        def add(z, carry):
            for y in range(2):
                for x in range(2):
                    chunk(p, h)[core, z, y, x] += rc[p % 2, h, z, y, x]
            return carry

        lax.fori_loop(0, 4, add, 0)
        begin(step_1(p, h))
        if p < 4:
            pl.semaphore_signal(credit.at[p % 2, h], inc=1, device_id=(partner,), device_id_type=MESH)

    def end_1(p, h):
        finish_steps(step_1(p, h))
        mine, way = chunk(p, h), route(p, h)
        if way[0] == "z":
            def add(y, carry):
                for x in range(2):
                    total = mine[core, zz, y, x].astype(F32)
                    for i in range(3):
                        total += rw[z_slot[(p, h)], i, y, x].astype(F32)
                    mine[core, zz, y, x] = total.astype(BF16)
                return carry

            lax.fori_loop(0, 2, add, 0)
        else:
            def add(z, carry):
                for i in range(2):
                    if way == "yxz":
                        mine[core, z, yy, i] += ra[p, h, z, i]
                    else:
                        mine[core, z, i, xx] += ra[p, h, z, i]
                return carry

            lax.fori_loop(0, 4, add, 0)
        begin(step_2(p, h))

    def end_2(p, h):
        finish_steps(step_2(p, h))
        mine = chunk(p, h)
        way = route(p, h)
        if way[0] == "z":
            for i in range(2):
                if way == "zyx":
                    mine[core, zz, yy, i] += rb[p, h, i]
                else:
                    mine[core, zz, i, xx] += rb[p, h, i]
        else:
            def add(z, carry):
                mine[core, z, yy, xx] += rb[p, h, z]
                return carry

            lax.fori_loop(0, 4, add, 0)
        begin(step_3(p, h))

    outs = []

    def end_3(p, h):
        finish_steps(step_3(p, h))
        total = chunk(p, h)[core, zz, yy, xx].astype(F32)
        for i in range(1 if route(p, h)[0] == "z" else 3):
            total += rz[p, h, i].astype(F32)
        parts[p, h] = total
        at = WIDE * h
        if p < 2:
            targets = [wbg.at[pl.ds(48 * p, 48), pl.ds(at, WIDE)]]
        elif p < 4:
            at += (p - 2) * 2 * D
            targets = [wig.at[:, pl.ds(at, WIDE)], wig.at[:, pl.ds(at + D, WIDE)]]
        else:
            targets = [ref.at[:, pl.ds(at, WIDE)] for ref in ((wvg, wog) if p == 4 else (wqg, wkg))]
        rows = 48 // len(targets)
        for i, target in enumerate(targets):
            outs.append(pltpu.make_async_copy(parts.at[p, h, pl.ds(rows * i, rows)], target, part_sem.at[p, h, i]))
            outs[-1].start()

    def store_grad(p, h, grad):
        for i in range(32):
            chunk(p, h)[i % 2, i // 8, (i // 4) % 2, (i // 2) % 2] = grad[i]

    def back_grad(p, h):
        left = jnp.concatenate([actT[96 * i + 48 * p:96 * i + 48 * p + 48, :] for i in range(32)], axis=0)
        grad = dot_nn(left, ml[:, WIDE * h:WIDE * h + WIDE]).astype(BF16)
        store_grad(p, h, grad.reshape(32, 48, WIDE))

    def pair_grad(p, h, left_0, right_0, left_1, right_1):
        cols = pl.ds(WIDE * h, WIDE)
        grad_0 = dot_nn(left_0[...], right_0[:, cols]).reshape(32, 24, WIDE)
        grad_1 = dot_nn(left_1[...], right_1[:, cols]).reshape(32, 24, WIDE)
        store_grad(p, h, jnp.concatenate([grad_0, grad_1], axis=1).astype(BF16))

    def in_grad(p, h):
        at = (p - 2) * 2 * D
        pair_grad(p, h, mlT, gp.at[:, pl.ds(at, D)], mlT, gp.at[:, pl.ds(at + D, D)])

    def inner_grad(t):
        cols = pl.ds(t * D, D)
        weight = wb_tile(t)
        tmp_a[...] = dot_nt(ml[0:256, :], weight)
        tmp_b[0:224, :] = dot_nt(ml[256:480, :], weight)
        total = zero8
        for ref, start, size in ((tmp_a, 0, 256), (tmp_b, 256, 224)):
            for at, count in blocks(0, size, 16):
                rows = pl.ds(start + at, count)
                rounded = (ref[at:at + count, :] * gp[rows, cols].astype(F32)).astype(BF16)
                gp[rows, cols] = rounded
                total = total + fold8(rounded.astype(F32))
        vec[8 + t:9 + t, :] = jnp.sum(total, axis=0, keepdims=True)

    def middle_grad(t):
        cols = pl.ds(t * D, D)
        n2[...] += dot_nt(gp[:, cols], wi[:, cols])

    def attn_norm_back():
        def block(i, sums):
            rows = pl.ds(pl.multiple_of(i * 32, 32), 32)
            upstream, unit = n2[rows, :], n1[rows, :]
            scaled = upstream * gain1
            hidden_grad = r1[rows, :] * (
                scaled
                - jnp.mean(scaled, axis=-1, keepdims=True)
                - unit * jnp.mean(scaled * unit, axis=-1, keepdims=True)
            )
            n1[rows, :] = hidden_grad
            rounded = hidden_grad.astype(BF16)
            ml[rows, :] = rounded
            return (
                sums[0] + fold8(upstream * unit), sums[1] + fold8(upstream), sums[2] + fold8(rounded.astype(F32)),
            )

        sums = lax.fori_loop(0, 15, block, (zero8, zero8, zero8))
        vec[2:3, :] = jnp.sum(sums[2], axis=0, keepdims=True)
        vec[3:4, :] = jnp.sum(sums[0], axis=0, keepdims=True)
        vec[4:5, :] = jnp.sum(sums[1], axis=0, keepdims=True)

    def context_grad():
        c_s[...] = dot_nt(ml[...], wo[...]).astype(BF16)

    def query_slot_back():
        q_rows, k_rows, v_rows = spread(q_s[0:32, :]), k_s[0:32, :], v_s[0:32, :]
        dc_rows = spread(c_s[0:32, :])
        soft = pq_s[...]
        dp = dot_nt(v_rows, dc_rows)
        soft_f = soft.astype(F32)
        ds = (soft_f * (dp - jnp.sum(soft_f * dp, axis=0, keepdims=True))).astype(BF16)
        v_s[0:32, :] = dot_nn(soft, dc_rows).astype(BF16)
        k_s[0:32, :] = dot_nn(ds, q_rows).astype(BF16)
        q_s[0:32, :] = (0.125 * gather_heads(dot_tn(ds, k_rows))).astype(BF16)

    def attend_back_pair(pair):
        lanes = pl.ds(pl.multiple_of(pair * 128, 128), 128)
        for slot in range(2):
            low_at = 12 * slot
            rows = pl.ds(32 + 208 * slot, WIN)
            keys, queries, values = k_s[rows, lanes], q_s[rows, lanes], v_s[rows, lanes]
            inside = ((key_at >= low_at) & (key_at < low_at + SLOT)).astype(BF16)
            upstream = c_s[rows, lanes] * inside
            keys_t = keys.T
            parts, dv, dk = [], 0.0, 0.0
            for h in range(2):
                p = p_s[slot, 2 * pair + h]
                dc = upstream * half[h]
                dp = dot_nt(values, dc)
                pf = p.astype(F32)
                ds = (pf * (dp - jnp.sum(pf * dp, axis=0, keepdims=True))).astype(BF16)
                dv += dot_nn(p, dc)
                dk += dot_nn(ds, queries * half[h])
                parts.append(dot_nn(keys_t, ds)[64 * h:64 * h + 64, :])
            dq = 0.125 * jnp.concatenate(parts, axis=0).T
            for ref, new in ((q_s, dq), (k_s, dk), (v_s, dv)):
                if slot == 0:
                    ref[32:240, lanes] = new[0:208].astype(BF16)
                    old = ref[240:272, lanes].astype(F32)
                    ref[240:272, lanes] = jnp.where(iota((32, 128), 0) < 12, new[208:240], old).astype(BF16)
                else:
                    old = ref[240:256, lanes].astype(F32)
                    ref[240:256, lanes] = jnp.where(iota((16, 128), 0) >= 12, new[0:16], old).astype(BF16)
                    ref[256:480, lanes] = new[16:240].astype(BF16)

    def attend_back(first, count):
        def step(i, carry):
            attend_back_pair(first + i)
            return carry

        lax.fori_loop(0, count, step, 0)

    def column_sum(ref):
        def step(i, total):
            return total + fold8(ref[pl.ds(pl.multiple_of(i * 32, 32), 32), :].astype(F32))

        return jnp.sum(lax.fori_loop(0, 15, step, zero8), axis=0, keepdims=True)

    def column_sums():
        vec[0:1, :] = column_sum(q_s)
        vec[1:2, :] = column_sum(v_s)

    def token_grad(grads, weight):
        n1[...] += dot_nt(grads[...], weight[...])

    out_qg = pltpu.make_async_copy(n1.at[0:32, :], qtg_h, out_sem.at[2])
    out_pg = pltpu.make_async_copy(n1.at[32:472, :], ptg_h, out_sem.at[3])

    def send_tokens():
        out_qg.start()
        out_pg.start()

    def vec_step(i):
        return remote(vec, vecr.at[i], v_send.at[i], v_recv.at[i], (partner, x_peer, y_peer)[i])

    def vec_part(whole, to):
        device = to * 8 + plane
        narrow = pltpu.roll(whole[0:8], D - 24 * device, 1)[:, 0:128]
        wide = pltpu.roll(whole[8:16], D - 96 * plane, 1)[:, 0:128]
        wide = jnp.sum(jnp.where(iota((8, 128), 0) == to, wide, 0.0), axis=0, keepdims=True)
        return jnp.concatenate([narrow, wide, jnp.zeros((7, 128), F32)], axis=0)

    def vec_z():
        return [
            remote(
                vecs.at[hop - 1], vecz.at[hop - 1], v_send.at[2 + hop], v_recv.at[2 + hop],
                lax.rem(zz + hop, 4) * 8 + plane,
            )
            for hop in range(1, 4)
        ]

    def vec_on(i):
        if i > 0:
            vec_step(i - 1).wait()
            vec[...] += vecr[i - 1]
        if i < 3:
            vec_step(i).start()
        else:
            whole = vec[...]
            for hop in range(1, 4):
                vecs[hop - 1] = vec_part(whole, lax.rem(zz + hop, 4))
            begin(vec_z())

    def vec_end():
        finish_steps(vec_z())
        part = vec_part(vec[...], zz) + vecz[0] + vecz[1] + vecz[2]
        small_o[0:9, :] = part[0:9]
        outs.append(pltpu.make_async_copy(small_o, small_h, out_sem.at[4]))
        outs[-1].start()

    pieces_of = {
        "wback": back_grad, "dinner": inner_grad, "win": in_grad, "dmid": middle_grad, "lnback": attn_norm_back,
        "dctx": context_grad, "qslot": query_slot_back, "attn": attend_back, "sums": column_sums,
        "wvo": lambda h: pair_grad(4, h, xT, v_s, cT, ml), "wqk": lambda h: pair_grad(5, h, xT, q_s, xT, k_s),
        "tq": lambda: token_grad(q_s, wq), "tk": lambda: token_grad(k_s, wk), "tv": lambda: token_grad(v_s, wv),
        "tout": send_tokens, "vec": vec_on, "vecend": vec_end,
        "c": start_c, "ec": end_c, "e1": end_1, "e2": end_2, "e3": end_3,
    }
    for name, *operands in ORDER:
        pieces_of[name](*operands)

    out_q.wait()
    out_p.wait()
    out_qg.wait()
    out_pg.wait()
    for out in outs:
        out.wait()


def hand_on_kernel(*refs):
    count = 10
    sources, small = refs[:count], refs[count]
    targets, vectors = refs[count + 1:2 * count + 1], refs[2 * count + 1:2 * count + 11]
    held, rest = refs[2 * count + 11:3 * count + 11], refs[3 * count + 11:]
    small_v, lines, in_sem, out_sem = rest[0], rest[1:11], rest[11], rest[12]
    whole = [(i, None) for i in range(count) if i != 3]
    pieces = [(3, pl.ds(at, size)) for at, size in blocks(0, 440, 112)] + whole
    into, out = [], []
    for at, (i, rows) in enumerate(pieces):
        source, kept, target = (ref if rows is None else ref.at[rows, :] for ref in (sources[i], held[i], targets[i]))
        into.append(pltpu.make_async_copy(source, kept, in_sem.at[at]))
        out.append(pltpu.make_async_copy(kept, target, out_sem.at[at]))
    last = pltpu.make_async_copy(small, small_v, in_sem.at[len(pieces)])
    last.start()
    for copy in into:
        copy.start()
    last.wait()
    for at, ref in enumerate(lines[:8]):
        ref[...] = small_v[at:at + 1, 0:24].reshape(24)
    lines[8][...] = small_v[8:9, 0:96].reshape(96)
    lines[9][...] = small_v[9:10, 0:1].reshape(1)
    for at, (line, vector) in enumerate(zip(lines, vectors)):
        out.append(pltpu.make_async_copy(line, vector, out_sem.at[len(pieces) + at]))
        out[-1].start()
    for first, second in zip(into, out):
        first.wait()
        second.start()
    for copy in out:
        copy.wait()


def on_device_small(*operands):
    (
        query_tokens, passage_tokens, query_lengths, passage_lengths, passage_valid, positives, negatives,
        teacher_margins, query_grad, passage_grad, weight_query, bias_query, weight_key, weight_value, bias_value,
        weight_out, bias_out, gain_attn, shift_attn, weight_in, bias_in, weight_back, bias_back, gain_ffn, shift_ffn,
    ) = operands
    hbm, far, smem = (pl.BlockSpec(memory_space=space) for space in (pl.ANY, pltpu.HBM, pltpu.SMEM))
    shape = jax.ShapeDtypeStruct
    slabs = (2, 2, 4, 2, 2, 48, D)
    large = (
        shape((32, D), BF16), shape((440, D), BF16), shape((32, D), F32), shape((440, D), F32), shape((24, D), F32),
        shape((24, D), F32), shape((24, D), F32), shape((24, D), F32), shape((24, FF), F32), shape((96, D), F32),
    )
    outs = pl.pallas_call(
        layer_kernel,
        out_shape=(
            *large, shape((16, 128), F32),
        ),
        in_specs=[
            hbm, hbm, far, smem, smem, far, far, far, hbm, hbm,
            *(hbm,) * 15,
        ],
        out_specs=(hbm,) * 11,
        scratch_shapes=[
            *(pltpu.VMEM((1,), kind) for kind in (jnp.int32, jnp.int32, jnp.int32, F32)),
            *(pltpu.VMEM((size,), BF16) for size in (D, D, D, D, D, FF, D, D, D)),
            pltpu.VMEM((D, D), BF16), pltpu.VMEM((D, D), BF16), pltpu.VMEM((D, D), BF16), pltpu.VMEM((D, D), BF16),
            pltpu.VMEM((D, FF), BF16), pltpu.VMEM((3, 2, 2, 4, 2, 2, 48, WIDE), BF16),
            pltpu.VMEM((440, D), BF16), pltpu.VMEM((ROWS, D), BF16), pltpu.VMEM((D, ROWS), BF16),
            pltpu.VMEM((ROWS, D), BF16), pltpu.VMEM((ROWS, D), BF16), pltpu.VMEM((ROWS, D), BF16),
            pltpu.VMEM((2, 12, WIN, WIN), BF16), pltpu.VMEM((32, 384), BF16),
            pltpu.VMEM((ROWS, D), BF16), pltpu.VMEM((D, ROWS), BF16),
            pltpu.VMEM((ROWS, D), F32), pltpu.VMEM((ROWS, D), F32), pltpu.VMEM((ROWS, 1), F32), pltpu.VMEM((ROWS, 1), F32),
            pltpu.VMEM((ROWS, D), BF16), pltpu.VMEM((D, ROWS), BF16),
            pltpu.VMEM((256, D), BF16), pltpu.VMEM((256, D), BF16), pltpu.VMEM((FF, ROWS), BF16),
            pltpu.VMEM((256, D), F32), pltpu.VMEM((256, D), F32),
            pltpu.VMEM((ROWS, FF), BF16),
            pltpu.VMEM((32, D), BF16), pltpu.VMEM((440, D), BF16), pltpu.VMEM((32, D), BF16), pltpu.VMEM((440, D), BF16),
            pltpu.VMEM((1024, 128), BF16), pltpu.VMEM((1024, 128), F32),
            pltpu.VMEM((16, D), F32), pltpu.VMEM((3, 16, D), F32), pltpu.VMEM((3, 16, 128), F32), pltpu.VMEM((3, 16, 128), F32),
            pltpu.VMEM((16, 128), F32), pltpu.VMEM((6, 3, 48, WIDE), F32),
            pltpu.VMEM((4, 3, 2, 4, 2, 2, 48, WIDE), BF16),
            pltpu.VMEM((2, 3, 4, 2, 2, 48, WIDE), BF16), pltpu.VMEM((6, 3, 4, 2, 48, WIDE), BF16),
            pltpu.VMEM((6, 3, 4, 48, WIDE), BF16), pltpu.VMEM((6, 3, 3, 48, WIDE), BF16),
            pltpu.VMEM((sum(way[0] == "z" for way in ROUTE), 3, 2, 2, 48, WIDE), BF16),
            pltpu.SemaphoreType.DMA((32,)), pltpu.SemaphoreType.DMA((5,)), pltpu.SemaphoreType.DMA((6, 3, 2)),
            pltpu.SemaphoreType.DMA((16,)), pltpu.SemaphoreType.DMA((16,)),
            pltpu.SemaphoreType.DMA((6, 3)), pltpu.SemaphoreType.DMA((6, 3)),
            pltpu.SemaphoreType.DMA((6, 3)), pltpu.SemaphoreType.DMA((6, 3)),
            pltpu.SemaphoreType.DMA((6, 3)), pltpu.SemaphoreType.DMA((6, 3)),
            pltpu.SemaphoreType.DMA((6, 3, 3)), pltpu.SemaphoreType.DMA((6, 3, 3)),
            pltpu.SemaphoreType.DMA((6,)), pltpu.SemaphoreType.DMA((6,)),
            pltpu.SemaphoreType.REGULAR((2, 3)),
        ],
        compiler_params=pltpu.CompilerParams(
            collective_id=0, has_side_effects=True, vmem_limit_bytes=64 * 1024 * 1024 - 65536,
        ),
        name="encoder_layer",
    )(
        query_tokens, passage_tokens, query_lengths, passage_lengths, passage_valid, positives, negatives,
        teacher_margins, query_grad, passage_grad, weight_query, bias_query, weight_key, weight_value, bias_value,
        weight_out, bias_out, gain_attn, shift_attn, weight_in, bias_in, weight_back.reshape(slabs), bias_back,
        gain_ffn, shift_ffn,
    )
    done = pl.pallas_call(
        hand_on_kernel,
        out_shape=large + (shape((24,), F32),) * 8 + (shape((96,), F32), shape((1,), F32)),
        in_specs=[hbm] * 11,
        out_specs=(hbm,) * 20,
        scratch_shapes=[pltpu.VMEM(out.shape, out.dtype) for out in large]
        + [pltpu.VMEM((16, 128), F32)] + [pltpu.VMEM((size,), F32) for size in (24,) * 8 + (96, 1)]
        + [pltpu.SemaphoreType.DMA((24,)), pltpu.SemaphoreType.DMA((24,))],
        name="hand_on",
    )(*outs)
    qout, pout, qtg, ptg, wqg, wkg, wvg, wog, wig, wbg, bqg, bvg, bog, gag, sag, bbg, gfg, sfg, big, loss = done
    return (
        qout, pout, loss, qtg, ptg, wqg, bqg, wkg, wvg, bvg, wog, bog, gag, sag, wig, big, wbg, bbg, gfg, sfg,
    )


def solution(mesh):
    return jax.shard_map(
        on_device_small if mesh.shape["dp"] == 32 else on_device,
        mesh=mesh,
        in_specs=(
            P("dp", None),
            P("dp", None),
            P("dp"),
            P("dp"),
            P("dp"),
            P("dp"),
            P("dp"),
            P("dp"),
            P("dp", None),
            P("dp", None),
            P(),
            P(),
            P(),
            P(),
            P(),
            P(),
            P(),
            P(),
            P(),
            P(),
            P(),
            P(),
            P(),
            P(),
            P(),
        ),
        out_specs=(
            P("dp", None),
            P("dp", None),
            P("dp"),
            P("dp", None),
            P("dp", None),
            P("dp", None),
            P("dp"),
            P("dp", None),
            P("dp", None),
            P("dp"),
            P("dp", None),
            P("dp"),
            P("dp"),
            P("dp"),
            P("dp", None),
            P("dp"),
            P("dp", None),
            P("dp"),
            P("dp"),
            P("dp"),
        ),
        check_vma=False,
    )
```

profile of v0, /device:TPU:0, one launch (start us, length us, event | category | flops | bytes accessed | tf_op | source)
XLA Modules:
  0.0 104.5 jit_solution(10423618483577535520)
XLA Ops:
  3.2 97.8 %encoder_layer.1 = (bf16[32,768]{1,0:T(8,128)(2,1)}, bf16[440,768]{1,0:T(8,128)(2,1)}, f32[32,768]{1,0:T(8,128)}, f32[440,768]{1,0:T(8,128)}, f32[24,768]{1,0:T(...) custom-call(bf16[32,768]{1,0:T(8,128)(2,1)} %qtok.1, ...), custom_call_target="tpu_custom_call" | custom-call | tf_op jit(solution)/shard_map/encoder_layer/pallas_call | solution.py:1205
  101.1 3.2 %hand_on.1 = (bf16[32,768]{1,0:T(8,128)(2,1)}, bf16[440,768]{1,0:T(8,128)(2,1)}, f32[32,768]{1,0:T(8,128)}, f32[440,768]{1,0:T(8,128)}, f32[24,768]{1,0:T(8,128)...) custom-call(bf16[32,768]{1,0:T(8,128)(2,1)} %get-tuple-element.51.re, ...), custom_call_target="tpu_custom_call" | custom-call | tf_op jit(solution)/shard_map/hand_on/pallas_call | solution.py:1256
where the time goes:
time: 105 us; the launch traced here: 104 us
  Pallas kernels  101 us (96%)
  between operations  3.43 us (3%)
    pallas_call x1, Pallas kernels, on_device_small(): pl.pallas_call(layer_kernel, out_shape=(*large, shape((16, 128), F32)), i...  97.8 us
    pallas_call x1, Pallas kernels, on_device_small(): pl.pallas_call(hand_on_kernel, out_shape=large + (shape((24,), F32),) * 8...  3.17 us

commit v1 on v0

--- a/solution.py
+++ b/solution.py
@@ -459,8 +459,8 @@
     return ref[pl.ds(start, size)].astype(F32).reshape(1, size)
 
 
-def one(ref):
-    return ref[...].reshape(1, 1)
+def item(ref, at):
+    return ref[...].reshape(1, 2)[:, at:at + 1]
 
 
 def blocks(start, stop, size):
@@ -477,35 +477,35 @@
 
 WIDE = 256
 ROUTE = (
-    "xyz", "yxz", "zyx", "xyz", "zxy", "zyx", "yxz", "xyz", "yxz", "xyz", "yxz", "xyz", "yxz", "xyz", "yxz", "xyz",
+    "xyz", "zyx", "zxy", "yxz", "xyz", "zyx", "yxz", "xyz", "yxz", "xyz", "yxz", "xyz", "yxz", "xyz", "yxz", "xyz",
     "yxz", "xyz",
 )
 ORDER = (
     ("wback", 0, 0), ("c", 0, 0), ("wback", 0, 1), ("c", 0, 1), ("wback", 0, 2), ("c", 0, 2), ("wback", 1, 0),
-    ("c", 1, 0), ("wback", 1, 1), ("c", 1, 1), ("wback", 1, 2), ("c", 1, 2), ("dinner", 0), ("ec", 0, 0),
-    ("dinner", 1), ("ec", 0, 2), ("win", 2, 0), ("ec", 0, 1), ("c", 2, 0), ("win", 2, 1), ("ec", 1, 0), ("c", 2, 1),
-    ("win", 2, 2), ("ec", 1, 2), ("ec", 1, 1), ("c", 2, 2), ("dinner", 2), ("dinner", 3), ("win", 3, 0), ("c", 3, 0),
-    ("ec", 2, 0), ("win", 3, 1), ("ec", 2, 1), ("c", 3, 1), ("win", 3, 2), ("c", 3, 2), ("dmid", 0), ("dmid", 1),
-    ("ec", 2, 2), ("dmid", 2), ("dmid", 3), ("lnback",), ("dctx",), ("ec", 3, 1), ("ec", 3, 0), ("qslot",),
-    ("e1", 1, 0), ("attn", 0, 1), ("ec", 3, 2), ("attn", 1, 4), ("e1", 0, 2), ("e1", 2, 2), ("attn", 5, 1),
-    ("sums",), ("wvo", 0), ("c", 4, 0), ("e1", 0, 1), ("e1", 2, 0), ("e1", 0, 0), ("wvo", 1), ("c", 4, 1),
-    ("wvo", 2), ("e1", 3, 1), ("c", 4, 2), ("vec", 0), ("e1", 2, 1), ("ec", 4, 0), ("wqk", 0), ("c", 5, 0),
-    ("ec", 4, 1), ("e2", 2, 2), ("e1", 3, 0), ("ec", 4, 2), ("e2", 0, 0), ("wqk", 1), ("e1", 3, 2), ("e2", 0, 1),
-    ("c", 5, 1), ("e2", 1, 0), ("vec", 1), ("wqk", 2), ("c", 5, 2), ("e2", 3, 1), ("e1", 4, 0), ("e2", 2, 1),
-    ("ec", 5, 2), ("e1", 4, 1), ("ec", 5, 1), ("e2", 2, 0), ("e3", 2, 2), ("e1", 4, 2), ("e2", 3, 0), ("ec", 5, 0),
-    ("e3", 0, 1), ("e2", 4, 0), ("e1", 5, 2), ("tq",), ("e3", 2, 1), ("e2", 3, 2), ("e3", 2, 0), ("e2", 4, 2),
-    ("e3", 3, 1), ("e1", 1, 2), ("e1", 1, 1), ("e2", 4, 1), ("e1", 5, 1), ("vec", 2), ("e1", 5, 0), ("e2", 5, 2),
-    ("e3", 3, 2), ("e3", 1, 0), ("vec", 3), ("e2", 5, 1), ("e3", 0, 0), ("tk",), ("e3", 4, 0), ("e2", 0, 2),
-    ("e2", 5, 0), ("e3", 4, 1), ("e2", 1, 1), ("e3", 4, 2), ("e2", 1, 2), ("e3", 1, 2), ("e3", 5, 1), ("e3", 3, 0),
-    ("vecend",), ("tv",), ("tout",), ("e3", 5, 2), ("e3", 1, 1), ("e3", 0, 2), ("e3", 5, 0),
+    ("c", 1, 0), ("wback", 1, 1), ("ec", 0, 0), ("c", 1, 1), ("wback", 1, 2), ("ec", 0, 1), ("c", 1, 2),
+    ("dinner", 0), ("ec", 1, 0), ("dinner", 1), ("win", 2, 0), ("c", 2, 0), ("ec", 1, 2), ("win", 2, 1),
+    ("ec", 0, 2), ("ec", 1, 1), ("c", 2, 1), ("win", 2, 2), ("ec", 2, 0), ("c", 2, 2), ("dinner", 2), ("dinner", 3),
+    ("ec", 2, 1), ("win", 3, 0), ("c", 3, 0), ("ec", 2, 2), ("win", 3, 1), ("c", 3, 1), ("win", 3, 2), ("e1", 0, 0),
+    ("c", 3, 2), ("dmid", 0), ("ec", 3, 0), ("e1", 1, 0), ("dmid", 1), ("dmid", 2), ("dmid", 3), ("lnback",),
+    ("dctx",), ("e1", 2, 0), ("qslot",), ("attn", 0, 1), ("e1", 2, 1), ("ec", 3, 1), ("attn", 1, 1), ("e1", 2, 2),
+    ("attn", 2, 4), ("e2", 2, 1), ("e1", 1, 1), ("ec", 3, 2), ("sums",), ("wvo", 0), ("c", 4, 0), ("wvo", 1),
+    ("c", 4, 1), ("wvo", 2), ("e1", 3, 0), ("e1", 3, 1), ("c", 4, 2), ("wqk", 0), ("ec", 4, 0), ("e2", 1, 1),
+    ("ec", 4, 2), ("e2", 0, 0), ("e2", 2, 2), ("c", 5, 0), ("ec", 4, 1), ("wqk", 1), ("e1", 3, 2), ("vec", 0),
+    ("e2", 2, 0), ("c", 5, 1), ("e2", 3, 0), ("wqk", 2), ("c", 5, 2), ("e1", 0, 1), ("ec", 5, 2), ("e1", 4, 1),
+    ("e3", 1, 1), ("e1", 4, 0), ("e2", 3, 1), ("e1", 4, 2), ("ec", 5, 1), ("e1", 1, 2), ("vec", 1), ("e3", 0, 0),
+    ("e2", 1, 0), ("e2", 3, 2), ("ec", 5, 0), ("e1", 5, 2), ("e2", 4, 0), ("tq",), ("e2", 4, 1), ("e1", 5, 1),
+    ("e2", 4, 2), ("e2", 0, 1), ("vec", 2), ("e3", 2, 1), ("tk",), ("e1", 5, 0), ("e2", 5, 2), ("e3", 3, 0),
+    ("e3", 3, 2), ("e1", 0, 2), ("vec", 3), ("e3", 1, 0), ("e2", 5, 1), ("e3", 2, 2), ("e2", 5, 0), ("e2", 0, 2),
+    ("e2", 1, 2), ("e3", 4, 1), ("e3", 0, 2), ("e3", 5, 2), ("tv",), ("tout",), ("e3", 0, 1), ("vecend",),
+    ("e3", 4, 0), ("e3", 2, 0), ("e3", 1, 2), ("e3", 3, 1), ("e3", 5, 1), ("e3", 4, 2), ("e3", 5, 0),
 )
 
 
 def layer_kernel(
-    qtok, ptok, qlen_h, plen, pvalid, pos_h, neg_h, margin_h, qgrad, pgrad,
+    qtok, ptok, qlen, plen_h, pvalid_h, pos, neg, margin, qgrad, pgrad,
     wq_h, bq_h, wk_h, wv_h, bv_h, wo_h, bo_h, ga_h, sa_h, wi_h, bi_h, wb_h, bb_h, gf_h, sf_h,
     qout_h, pout_h, qtg_h, ptg_h, wqg, wkg, wvg, wog, wig, wbg, small_h,
-    qlen, pos, neg, margin, bq, bv, bo, ga, sa, bi, bb, gf, sf, wq, wk, wv, wo, wi, wb, pstage, x_s, xT, q_s, k_s, v_s, p_s, pq_s, c_s, cT, n1, n2, r1, r2,
+    plen, pvalid, bq, bv, bo, ga, sa, bi, bb, gf, sf, wq, wk, wv, wo, wi, wb, pstage, x_s, xT, q_s, k_s, v_s, p_s, pq_s, c_s, cT, n1, n2, r1, r2,
     ml, mlT, act_a, act_b, actT, tmp_a, tmp_b, gp, qg_s, pg_s, qo_s, po_s, ex, ex_f, vec, vecr, vecs, vecz, small_o, parts,
     g_s, rc, ra, rb, rz, rw,
     load_sem, out_sem, part_sem, ex_send, ex_recv, c_send, c_recv, a_send, a_recv, b_send, b_recv,
@@ -531,11 +531,14 @@
     load("ptok", ptok, pstage)
     load("qtok", qtok, qo_s)
     load("wq", wq_h, wq)
+    vectors = (
+        (plen_h, plen), (pvalid_h, pvalid), (bq_h, bq), (bv_h, bv), (bo_h, bo), (ga_h, ga), (sa_h, sa), (bi_h, bi),
+        (bb_h, bb), (gf_h, gf), (sf_h, sf),
+    )
+    for at, (source, target) in enumerate(vectors):
+        load("vec" + str(at), source, target)
     load("wk", wk_h, wk)
     load("wv", wv_h, wv)
-    vectors = ((qlen_h, qlen), (pos_h, pos), (neg_h, neg), (margin_h, margin), (bq_h, bq), (bv_h, bv), (bo_h, bo), (ga_h, ga), (sa_h, sa), (bi_h, bi), (bb_h, bb), (gf_h, gf), (sf_h, sf))
-    for at, (source, target) in enumerate(vectors):
-        load("vec" + str(at), source, target)
 
     barrier = pltpu.get_barrier_semaphore()
     for hop in range(1, 16):
@@ -561,7 +564,12 @@
         loads["vec" + str(at)].wait()
     load("wo", wo_h, wo)
     load("wi", wi_h, wi)
-    q_s[...] = ((dot_nn(x_s[...], wq[...]) + row_of(bq)).astype(BF16) * 0.125).astype(BF16)
+
+    def project_queries(start, stop):
+        rows = pl.ds(start, stop - start)
+        q_s[rows, :] = ((dot_nn(x_s[rows, :], wq[...]) + row_of(bq)).astype(BF16) * 0.125).astype(BF16)
+
+    project_queries(0, 256)
     loads["wk"].wait()
     k_s[...] = dot_nn(x_s[...], wk[...]).astype(BF16)
     loads["wv"].wait()
@@ -581,11 +589,19 @@
         return jnp.sum(stacked.reshape(12, 32, D) * head_mask, axis=0)
 
     raw = dot_nt(k_s[0:32, :], spread(q_s[0:32, :]))
-    raw = jnp.where(iota((32, 384), 0) < one(qlen), raw, NEG)
+    raw = jnp.where(iota((32, 384), 0) < qlen[0], raw, NEG)
     soft = jnp.exp(raw - jnp.max(raw, axis=0, keepdims=True))
     soft = (soft * (1.0 / jnp.sum(soft, axis=0, keepdims=True))).astype(BF16)
     pq_s[...] = soft
     c_s[0:32, :] = gather_heads(dot_tn(soft, v_s[0:32, :])).astype(BF16)
+
+    by_head = (q_s[240:256, :].astype(F32)[None] * head_mask).astype(BF16).reshape(192, D)
+    raw = dot_nt(by_head, k_s[240:480, :])
+    key_lane = iota((1, WIN), 1)
+    raw = jnp.where((key_lane >= 12) & (key_lane < 12 + item(plen, 1)), raw, NEG)
+    soft = jnp.exp(raw - jnp.max(raw, axis=1, keepdims=True))
+    soft = (soft * (1.0 / jnp.sum(soft, axis=1, keepdims=True))).astype(BF16)
+    block = jnp.sum(dot_nn(soft, v_s[240:480, :]).reshape(12, 16, D) * head_mask, axis=0)
 
     lane = iota((1, 128), 1)
     half = ((lane < 64).astype(BF16), (lane >= 64).astype(BF16))
@@ -598,7 +614,7 @@
         rows = pl.ds(first_row, WIN)
         keys, queries = k_s[rows, lanes], q_s[rows, lanes]
         values_t = v_s[rows, lanes].T
-        allowed = (key_at >= low_at) & (key_at < low_at + plen[slot])
+        allowed = (key_at >= low_at) & (key_at < low_at + item(plen, slot))
         parts = []
         for h in range(2):
             scores = jnp.where(allowed, dot_nt(keys, queries * half[h]), NEG)
@@ -614,12 +630,17 @@
         c_s[240:256, lanes] = jnp.where(iota((16, 128), 0) >= 12, context[0:16], old).astype(BF16)
         c_s[256:480, lanes] = context[16:240].astype(BF16)
 
-    def both_slots(pair, carry):
-        attend(pair, 0)
-        attend(pair, 1)
-        return carry
-
-    lax.fori_loop(0, 6, both_slots, 0)
+    def attend_slot(slot):
+        def two_pairs(i, carry):
+            attend(2 * i, slot)
+            attend(2 * i + 1, slot)
+            return carry
+
+        lax.fori_loop(0, 3, two_pairs, 0)
+
+    attend_slot(0)
+    old = c_s[240:256, :].astype(F32)
+    c_s[240:256, :] = jnp.where(iota((16, 1), 0) >= 12, block, old).astype(BF16)
 
     loads["wo"].wait()
     gain1, shift1, bias1 = row_of(ga), row_of(sa), row_of(bo)
@@ -698,11 +719,11 @@
     )
     lane_row = iota((1, 128), 1)
     meta = jnp.zeros((1, 128), F32)
-    margin_0 = jnp.zeros((1, 128), F32) + one(margin)
+    margin_0 = jnp.zeros((1, 128), F32) + margin[0]
     margin_1 = margin_0.astype(BF16).astype(F32)
     margin_2 = (margin_0 - margin_1).astype(BF16).astype(F32)
     for at, value in enumerate((
-        pvalid[0].astype(F32), pvalid[1].astype(F32), one(pos).astype(F32), one(neg).astype(F32),
+        item(pvalid, 0).astype(F32), item(pvalid, 1).astype(F32), pos[0].astype(F32), neg[0].astype(F32),
         margin_1, margin_2, margin_0 - margin_1 - margin_2,
     )):
         meta = jnp.where(lane_row == at, value, meta)
@@ -719,6 +740,8 @@
         ))
         sends[-1].start()
 
+    project_queries(256, 480)
+    attend_slot(1)
     forward_rows(256, 480)
     out_q = pltpu.make_async_copy(qo_s, qout_h, out_sem.at[0])
     out_p = pltpu.make_async_copy(po_s, pout_h, out_sem.at[1])
@@ -1195,7 +1218,7 @@
         teacher_margins, query_grad, passage_grad, weight_query, bias_query, weight_key, weight_value, bias_value,
         weight_out, bias_out, gain_attn, shift_attn, weight_in, bias_in, weight_back, bias_back, gain_ffn, shift_ffn,
     ) = operands
-    hbm, far, smem = (pl.BlockSpec(memory_space=space) for space in (pl.ANY, pltpu.HBM, pltpu.SMEM))
+    hbm, smem = (pl.BlockSpec(memory_space=space) for space in (pl.ANY, pltpu.SMEM))
     shape = jax.ShapeDtypeStruct
     slabs = (2, 2, 4, 2, 2, 48, D)
     large = (
@@ -1208,12 +1231,12 @@
             *large, shape((16, 128), F32),
         ),
         in_specs=[
-            hbm, hbm, far, smem, smem, far, far, far, hbm, hbm,
+            hbm, hbm, smem, hbm, hbm, smem, smem, smem, hbm, hbm,
             *(hbm,) * 15,
         ],
         out_specs=(hbm,) * 11,
         scratch_shapes=[
-            *(pltpu.VMEM((1,), kind) for kind in (jnp.int32, jnp.int32, jnp.int32, F32)),
+            pltpu.VMEM((2,), jnp.int32), pltpu.VMEM((2,), jnp.int32),
             *(pltpu.VMEM((size,), BF16) for size in (D, D, D, D, D, FF, D, D, D)),
             pltpu.VMEM((D, D), BF16), pltpu.VMEM((D, D), BF16), pltpu.VMEM((D, D), BF16), pltpu.VMEM((D, D), BF16),
             pltpu.VMEM((D, FF), BF16), pltpu.VMEM((3, 2, 2, 4, 2, 2, 48, WIDE), BF16),

time: 105 us -> 103 us (0.981)
  Pallas kernels: 101 us -> 98.9 us
    pallas_call x1, Pallas kernels: 97.8 us -> 95.8 us  [on_device_small(): pl.pallas_call(layer_kernel, out_shape=(*large, shape((16, 128), F32)), i...]
where the time goes in v1:
time: 103 us; the launch traced here: 102 us
  Pallas kernels  98.9 us (96%)
  between operations  3.43 us (3%)
    pallas_call x1, Pallas kernels, on_device_small(): pl.pallas_call(layer_kernel, out_shape=(*large, shape((16, 128), F32)), i...  95.8 us
    pallas_call x1, Pallas kernels, on_device_small(): pl.pallas_call(hand_on_kernel, out_shape=large + (shape((24,), F32),) * 8...  3.17 us

profile of v1, /device:TPU:0, one launch (start us, length us, event | category | flops | bytes accessed | tf_op | source)
XLA Modules:
  0.0 102.4 jit_solution(16292683187685925706)
XLA Ops:
  3.2 95.8 %encoder_layer.1 = (bf16[32,768]{1,0:T(8,128)(2,1)}, bf16[440,768]{1,0:T(8,128)(2,1)}, f32[32,768]{1,0:T(8,128)}, f32[440,768]{1,0:T(8,128)}, f32[24,768]{1,0:T(...) custom-call(bf16[32,768]{1,0:T(8,128)(2,1)} %qtok.1, ...), custom_call_target="tpu_custom_call" | custom-call | tf_op jit(solution)/shard_map/encoder_layer/pallas_call | solution.py:1228
  99.0 3.2 %hand_on.1 = (bf16[32,768]{1,0:T(8,128)(2,1)}, bf16[440,768]{1,0:T(8,128)(2,1)}, f32[32,768]{1,0:T(8,128)}, f32[440,768]{1,0:T(8,128)}, f32[24,768]{1,0:T(8,128)...) custom-call(bf16[32,768]{1,0:T(8,128)(2,1)} %get-tuple-element.51.re, ...), custom_call_target="tpu_custom_call" | custom-call | tf_op jit(solution)/shard_map/hand_on/pallas_call | solution.py:1279

commit v2 on v1

--- a/solution.py
+++ b/solution.py
@@ -477,28 +477,32 @@
 
 WIDE = 256
 ROUTE = (
-    "xyz", "zyx", "zxy", "yxz", "xyz", "zyx", "yxz", "xyz", "yxz", "xyz", "yxz", "xyz", "yxz", "xyz", "yxz", "xyz",
+    "xyz", "yxz", "ryx", "xyz", "rxy", "ryx", "yxz", "xyz", "yxz", "xyz", "yxz", "xyz", "yxz", "xyz", "yxz", "xyz",
     "yxz", "xyz",
 )
 ORDER = (
     ("wback", 0, 0), ("c", 0, 0), ("wback", 0, 1), ("c", 0, 1), ("wback", 0, 2), ("c", 0, 2), ("wback", 1, 0),
-    ("c", 1, 0), ("wback", 1, 1), ("ec", 0, 0), ("c", 1, 1), ("wback", 1, 2), ("ec", 0, 1), ("c", 1, 2),
-    ("dinner", 0), ("ec", 1, 0), ("dinner", 1), ("win", 2, 0), ("c", 2, 0), ("ec", 1, 2), ("win", 2, 1),
-    ("ec", 0, 2), ("ec", 1, 1), ("c", 2, 1), ("win", 2, 2), ("ec", 2, 0), ("c", 2, 2), ("dinner", 2), ("dinner", 3),
-    ("ec", 2, 1), ("win", 3, 0), ("c", 3, 0), ("ec", 2, 2), ("win", 3, 1), ("c", 3, 1), ("win", 3, 2), ("e1", 0, 0),
-    ("c", 3, 2), ("dmid", 0), ("ec", 3, 0), ("e1", 1, 0), ("dmid", 1), ("dmid", 2), ("dmid", 3), ("lnback",),
-    ("dctx",), ("e1", 2, 0), ("qslot",), ("attn", 0, 1), ("e1", 2, 1), ("ec", 3, 1), ("attn", 1, 1), ("e1", 2, 2),
-    ("attn", 2, 4), ("e2", 2, 1), ("e1", 1, 1), ("ec", 3, 2), ("sums",), ("wvo", 0), ("c", 4, 0), ("wvo", 1),
-    ("c", 4, 1), ("wvo", 2), ("e1", 3, 0), ("e1", 3, 1), ("c", 4, 2), ("wqk", 0), ("ec", 4, 0), ("e2", 1, 1),
-    ("ec", 4, 2), ("e2", 0, 0), ("e2", 2, 2), ("c", 5, 0), ("ec", 4, 1), ("wqk", 1), ("e1", 3, 2), ("vec", 0),
-    ("e2", 2, 0), ("c", 5, 1), ("e2", 3, 0), ("wqk", 2), ("c", 5, 2), ("e1", 0, 1), ("ec", 5, 2), ("e1", 4, 1),
-    ("e3", 1, 1), ("e1", 4, 0), ("e2", 3, 1), ("e1", 4, 2), ("ec", 5, 1), ("e1", 1, 2), ("vec", 1), ("e3", 0, 0),
-    ("e2", 1, 0), ("e2", 3, 2), ("ec", 5, 0), ("e1", 5, 2), ("e2", 4, 0), ("tq",), ("e2", 4, 1), ("e1", 5, 1),
-    ("e2", 4, 2), ("e2", 0, 1), ("vec", 2), ("e3", 2, 1), ("tk",), ("e1", 5, 0), ("e2", 5, 2), ("e3", 3, 0),
-    ("e3", 3, 2), ("e1", 0, 2), ("vec", 3), ("e3", 1, 0), ("e2", 5, 1), ("e3", 2, 2), ("e2", 5, 0), ("e2", 0, 2),
-    ("e2", 1, 2), ("e3", 4, 1), ("e3", 0, 2), ("e3", 5, 2), ("tv",), ("tout",), ("e3", 0, 1), ("vecend",),
-    ("e3", 4, 0), ("e3", 2, 0), ("e3", 1, 2), ("e3", 3, 1), ("e3", 5, 1), ("e3", 4, 2), ("e3", 5, 0),
+    ("c", 1, 0), ("ec", 0, 0), ("wback", 1, 1), ("ec", 0, 1), ("c", 1, 1), ("wback", 1, 2), ("ec", 0, 2),
+    ("c", 1, 2), ("dinner", 0), ("dinner", 1), ("win", 2, 0), ("c", 2, 0), ("ec", 1, 0), ("win", 2, 1), ("c", 2, 1),
+    ("win", 2, 2), ("c", 2, 2), ("ec", 1, 1), ("ec", 2, 0), ("dinner", 2), ("dinner", 3), ("e1", 0, 1),
+    ("win", 3, 0), ("c", 3, 0), ("win", 3, 1), ("e1", 0, 0), ("c", 3, 1), ("win", 3, 2), ("ec", 2, 1), ("ec", 1, 2),
+    ("c", 3, 2), ("dmid", 0), ("dmid", 1), ("ec", 2, 2), ("ec", 3, 1), ("e1", 0, 2), ("ec", 3, 0), ("dmid", 2),
+    ("dmid", 3), ("ec", 3, 2), ("lnback",), ("e2", 0, 1), ("dctx",), ("e1", 1, 0), ("e2", 0, 0), ("qslot",),
+    ("attn", 0, 1), ("e1", 2, 0), ("e1", 1, 1), ("attn", 1, 2), ("e1", 2, 1), ("attn", 3, 3), ("sums",),
+    ("e1", 3, 0), ("e1", 1, 2), ("wvo", 0), ("e1", 3, 1), ("c", 4, 0), ("vec", 0), ("wvo", 1), ("c", 4, 1),
+    ("e1", 2, 2), ("wvo", 2), ("e1", 3, 2), ("c", 4, 2), ("wqk", 0), ("c", 5, 0), ("wqk", 1), ("ec", 4, 1),
+    ("c", 5, 1), ("wqk", 2), ("e2", 2, 1), ("ec", 4, 2), ("e3", 0, 1), ("e2", 3, 0), ("e2", 2, 0), ("vec", 1),
+    ("e2", 3, 1), ("ec", 5, 1), ("e2", 1, 0), ("e2", 3, 2), ("ec", 5, 0), ("e2", 2, 2), ("e1", 4, 1), ("e1", 4, 2),
+    ("vec", 2), ("ec", 4, 0), ("c", 5, 2), ("tq",), ("e3", 3, 0), ("e1", 5, 1), ("ec", 5, 2), ("e2", 4, 1),
+    ("e1", 5, 0), ("vec", 3), ("e3", 0, 0), ("e2", 0, 2), ("e2", 5, 1), ("tk",), ("e2", 1, 2), ("e1", 4, 0),
+    ("e2", 4, 2), ("e3", 2, 0), ("e1", 5, 2), ("e2", 5, 0), ("e3", 3, 1), ("e2", 1, 1), ("e2", 4, 0), ("e3", 2, 2),
+    ("e2", 5, 2), ("e3", 1, 2), ("e3", 1, 1), ("e3", 4, 2), ("e3", 0, 2), ("e3", 4, 1), ("e4", 1, 1), ("e3", 2, 1),
+    ("vecend",), ("e3", 5, 1), ("e3", 5, 0), ("e3", 3, 2), ("tv",), ("tout",), ("e3", 4, 0), ("e3", 1, 0),
+    ("e4", 0, 2), ("e4", 1, 2), ("e3", 5, 2),
 )
+
+
+RELAYS = max(1, sum(way[0] == "r" for way in ROUTE))
 
 
 def layer_kernel(
@@ -507,9 +511,9 @@
     qout_h, pout_h, qtg_h, ptg_h, wqg, wkg, wvg, wog, wig, wbg, small_h,
     plen, pvalid, bq, bv, bo, ga, sa, bi, bb, gf, sf, wq, wk, wv, wo, wi, wb, pstage, x_s, xT, q_s, k_s, v_s, p_s, pq_s, c_s, cT, n1, n2, r1, r2,
     ml, mlT, act_a, act_b, actT, tmp_a, tmp_b, gp, qg_s, pg_s, qo_s, po_s, ex, ex_f, vec, vecr, vecs, vecz, small_o, parts,
-    g_s, rc, ra, rb, rz, rw,
+    g_s, rc, ra, rb, rz, rw, rw_mate, rw_far, rw_in,
     load_sem, out_sem, part_sem, ex_send, ex_recv, c_send, c_recv, a_send, a_recv, b_send, b_recv,
-    z_send, z_recv, v_send, v_recv, credit,
+    z_send, z_recv, r_send, v_send, v_recv, credit,
 ):
     me = lax.axis_index("dp")
     core = lax.rem(me, 2)
@@ -848,10 +852,14 @@
     def chunk(p, h):
         return g_s.at[p, h] if p < 4 else wb.at[h, p - 4]
 
-    z_slot = {}
+    z_slot, r_slot = {}, {}
     for at, way in enumerate(ROUTE):
-        if way[0] == "z":
-            z_slot[(at // 3, at % 3)] = len(z_slot)
+        for kind, slots in (("z", z_slot), ("r", r_slot)):
+            if way[0] == kind:
+                slots[(at // 3, at % 3)] = len(slots)
+    inner = (zz == 1) | (zz == 2)
+    mate = zz + 1 - 2 * lax.rem(zz, 2)
+    far = 2 - 2 * lax.div(zz, 2)
 
     def route(p, h):
         return ROUTE[3 * p + h]
@@ -882,9 +890,9 @@
 
     def step_2(p, h):
         mine, way = chunk(p, h), route(p, h)
-        if way == "zyx":
+        if way in ("zyx", "ryx"):
             away, target = mine.at[core, zz, 1 - yy], rb.at[p, h, 0:2]
-        elif way == "zxy":
+        elif way in ("zxy", "rxy"):
             away, target = mine.at[core, zz, :, 1 - xx], rb.at[p, h, 0:2]
         elif way == "xyz":
             away, target = mine.at[core, :, 1 - yy, xx], rb.at[p, h]
@@ -895,10 +903,10 @@
     def step_3(p, h):
         mine = chunk(p, h)
         way = route(p, h)
-        if way[0] == "z":
-            away = mine.at[core, zz, yy, 1 - xx] if way == "zyx" else mine.at[core, zz, 1 - yy, xx]
+        if way[0] in "zr":
+            away = mine.at[core, zz, yy, 1 - xx] if way[2] == "x" else mine.at[core, zz, 1 - yy, xx]
             return [remote(
-                away, rz.at[p, h, 0], a_send.at[p, h], a_recv.at[p, h], x_peer if way == "zyx" else y_peer,
+                away, rz.at[p, h, 0], a_send.at[p, h], a_recv.at[p, h], x_peer if way[2] == "x" else y_peer,
             )]
         return along_z(p, h, lambda to: mine.at[core, to, yy, xx], lambda i: rz.at[p, h, i])
 
@@ -909,6 +917,70 @@
     def finish_steps(steps):
         for step in steps:
             step.wait()
+
+    def mate_step(p, h):
+        return remote(
+            chunk(p, h).at[core, mate], rw_mate.at[r_slot[(p, h)]], z_send.at[p, h, 0], z_recv.at[p, h, 0],
+            mate * 8 + plane,
+        )
+
+    def far_step(p, h):
+        return remote(
+            chunk(p, h).at[core, pl.ds(far, 2)], rw_far.at[r_slot[(p, h)]], z_send.at[p, h, 1], z_recv.at[p, h, 1],
+            mate * 8 + plane,
+        )
+
+    def relay_step(p, h, i):
+        return remote(
+            chunk(p, h).at[core, far + i], rw_in.at[r_slot[(p, h)]], r_send.at[r_slot[(p, h)], i], z_recv.at[p, h, 2],
+            (far + i) * 8 + plane,
+        )
+
+    def start_relay(p, h):
+        mate_step(p, h).start()
+
+        @pl.when(jnp.logical_not(inner))
+        def _():
+            far_step(p, h).start()
+
+    def relay_on(p, h):
+        @pl.when(inner)
+        def _():
+            far_step(p, h).wait_recv()
+
+            def add(i, carry):
+                for y in range(2):
+                    for x in range(2):
+                        chunk(p, h)[core, far + i, y, x] += rw_far[r_slot[(p, h)], i, y, x]
+                return carry
+
+            lax.fori_loop(0, 2, add, 0)
+            for i in range(2):
+                relay_step(p, h, i).start()
+
+        @pl.when(jnp.logical_not(inner))
+        def _():
+            far_step(p, h).wait_send()
+
+    def end_relay(p, h):
+        mate_step(p, h).wait()
+        relay_step(p, h, 0).wait_recv()
+
+        @pl.when(inner)
+        def _():
+            for i in range(2):
+                relay_step(p, h, i).wait_send()
+
+        mine, at = chunk(p, h), r_slot[(p, h)]
+
+        def add(y, carry):
+            for x in range(2):
+                total = mine[core, zz, y, x].astype(F32) + rw_mate[at, y, x].astype(F32) + rw_in[at, y, x].astype(F32)
+                mine[core, zz, y, x] = total.astype(BF16)
+            return carry
+
+        lax.fori_loop(0, 2, add, 0)
+        begin(step_2(p, h))
 
     def start_c(p, h):
         if p >= 2:
@@ -925,7 +997,10 @@
             return carry
 
         lax.fori_loop(0, 4, add, 0)
-        begin(step_1(p, h))
+        if route(p, h)[0] == "r":
+            start_relay(p, h)
+        else:
+            begin(step_1(p, h))
         if p < 4:
             pl.semaphore_signal(credit.at[p % 2, h], inc=1, device_id=(partner,), device_id_type=MESH)
 
@@ -958,9 +1033,9 @@
         finish_steps(step_2(p, h))
         mine = chunk(p, h)
         way = route(p, h)
-        if way[0] == "z":
+        if way[0] in "zr":
             for i in range(2):
-                if way == "zyx":
+                if way[1] == "y":
                     mine[core, zz, yy, i] += rb[p, h, i]
                 else:
                     mine[core, zz, i, xx] += rb[p, h, i]
@@ -977,7 +1052,7 @@
     def end_3(p, h):
         finish_steps(step_3(p, h))
         total = chunk(p, h)[core, zz, yy, xx].astype(F32)
-        for i in range(1 if route(p, h)[0] == "z" else 3):
+        for i in range(1 if route(p, h)[0] in "zr" else 3):
             total += rz[p, h, i].astype(F32)
         parts[p, h] = total
         at = WIDE * h
@@ -1161,13 +1236,18 @@
         outs.append(pltpu.make_async_copy(small_o, small_h, out_sem.at[4]))
         outs[-1].start()
 
+    def serve(at, p, h):
+        relayed = route(p, h)[0] == "r"
+        ((relay_on, end_relay, end_2, end_3) if relayed else (end_1, end_2, end_3))[at](p, h)
+
     pieces_of = {
         "wback": back_grad, "dinner": inner_grad, "win": in_grad, "dmid": middle_grad, "lnback": attn_norm_back,
         "dctx": context_grad, "qslot": query_slot_back, "attn": attend_back, "sums": column_sums,
         "wvo": lambda h: pair_grad(4, h, xT, v_s, cT, ml), "wqk": lambda h: pair_grad(5, h, xT, q_s, xT, k_s),
         "tq": lambda: token_grad(q_s, wq), "tk": lambda: token_grad(k_s, wk), "tv": lambda: token_grad(v_s, wv),
         "tout": send_tokens, "vec": vec_on, "vecend": vec_end,
-        "c": start_c, "ec": end_c, "e1": end_1, "e2": end_2, "e3": end_3,
+        "c": start_c, "ec": end_c, "e1": lambda p, h: serve(0, p, h), "e2": lambda p, h: serve(1, p, h),
+        "e3": lambda p, h: serve(2, p, h), "e4": lambda p, h: serve(3, p, h),
     }
     for name, *operands in ORDER:
         pieces_of[name](*operands)
@@ -1256,13 +1336,15 @@
             pltpu.VMEM((4, 3, 2, 4, 2, 2, 48, WIDE), BF16),
             pltpu.VMEM((2, 3, 4, 2, 2, 48, WIDE), BF16), pltpu.VMEM((6, 3, 4, 2, 48, WIDE), BF16),
             pltpu.VMEM((6, 3, 4, 48, WIDE), BF16), pltpu.VMEM((6, 3, 3, 48, WIDE), BF16),
-            pltpu.VMEM((sum(way[0] == "z" for way in ROUTE), 3, 2, 2, 48, WIDE), BF16),
+            pltpu.VMEM((max(1, sum(way[0] == "z" for way in ROUTE)), 3, 2, 2, 48, WIDE), BF16),
+            pltpu.VMEM((RELAYS, 2, 2, 48, WIDE), BF16), pltpu.VMEM((RELAYS, 2, 2, 2, 48, WIDE), BF16),
+            pltpu.VMEM((RELAYS, 2, 2, 48, WIDE), BF16),
             pltpu.SemaphoreType.DMA((32,)), pltpu.SemaphoreType.DMA((5,)), pltpu.SemaphoreType.DMA((6, 3, 2)),
             pltpu.SemaphoreType.DMA((16,)), pltpu.SemaphoreType.DMA((16,)),
             pltpu.SemaphoreType.DMA((6, 3)), pltpu.SemaphoreType.DMA((6, 3)),
             pltpu.SemaphoreType.DMA((6, 3)), pltpu.SemaphoreType.DMA((6, 3)),
             pltpu.SemaphoreType.DMA((6, 3)), pltpu.SemaphoreType.DMA((6, 3)),
-            pltpu.SemaphoreType.DMA((6, 3, 3)), pltpu.SemaphoreType.DMA((6, 3, 3)),
+            pltpu.SemaphoreType.DMA((6, 3, 3)), pltpu.SemaphoreType.DMA((6, 3, 3)), pltpu.SemaphoreType.DMA((RELAYS, 2)),
             pltpu.SemaphoreType.DMA((6,)), pltpu.SemaphoreType.DMA((6,)),
             pltpu.SemaphoreType.REGULAR((2, 3)),
         ],

time: 103 us -> 100 us (0.971)
  Pallas kernels: 98.9 us -> 96.8 us
    pallas_call x1, Pallas kernels: 95.8 us -> 93.6 us  [on_device_small(): pl.pallas_call(layer_kernel, out_shape=(*large, shape((16, 128), F32)), i...]
where the time goes in v2:
time: 100 us
  Pallas kernels  96.8 us (97%)
  between operations  3.43 us (3%)
    pallas_call x1, Pallas kernels, on_device_small(): pl.pallas_call(layer_kernel, out_shape=(*large, shape((16, 128), F32)), i...  93.6 us
    pallas_call x1, Pallas kernels, on_device_small(): pl.pallas_call(hand_on_kernel, out_shape=large + (shape((24,), F32),) * 8...  3.17 us

profile of v2, /device:TPU:0, one launch (start us, length us, event | category | flops | bytes accessed | tf_op | source)
XLA Modules:
  0.0 100.2 jit_solution(1887358588243379119)
XLA Ops:
  3.2 93.6 %encoder_layer.1 = (bf16[32,768]{1,0:T(8,128)(2,1)}, bf16[440,768]{1,0:T(8,128)(2,1)}, f32[32,768]{1,0:T(8,128)}, f32[440,768]{1,0:T(8,128)}, f32[24,768]{1,0:T(...) custom-call(bf16[32,768]{1,0:T(8,128)(2,1)} %qtok.1, ...), custom_call_target="tpu_custom_call" | custom-call | tf_op jit(solution)/shard_map/encoder_layer/pallas_call | solution.py:1308
  96.9 3.2 %hand_on.1 = (bf16[32,768]{1,0:T(8,128)(2,1)}, bf16[440,768]{1,0:T(8,128)(2,1)}, f32[32,768]{1,0:T(8,128)}, f32[440,768]{1,0:T(8,128)}, f32[24,768]{1,0:T(8,128)...) custom-call(bf16[32,768]{1,0:T(8,128)(2,1)} %get-tuple-element.51.re, ...), custom_call_target="tpu_custom_call" | custom-call | tf_op jit(solution)/shard_map/hand_on/pallas_call | solution.py:1361

commit v3 on v2

--- a/solution.py
+++ b/solution.py
@@ -773,12 +773,8 @@
     zero8 = jnp.zeros((8, D), F32)
     sums = (zero8, zero8, zero8)
 
-    def middle_block(i, sums):
-        upstream = pg_s[pl.ds(pl.multiple_of(i * 32, 32), 32), :].astype(F32)
-        return ffn_norm_back(pl.multiple_of(32 + i * 32, 32), upstream, sums)
-
-    sums = lax.fori_loop(1, 6, middle_block, sums)
-    sums = lax.fori_loop(7, 13, middle_block, sums)
+    for i in (1, 2, 3, 4, 5, 7, 8, 9, 10, 11, 12):
+        sums = ffn_norm_back(32 + 32 * i, pg_s[32 * i:32 * i + 32, :].astype(F32), sums)
     last = jnp.concatenate([pg_s[416:440, :].astype(F32), jnp.zeros((8, D), F32)], axis=0)
     sums = ffn_norm_back(448, last, sums)
 

time: 100 us -> 99.7 us (level)
  no operation moved by 1% of the time
where the time goes in v3:
time: 99.7 us; the launch traced here: 99.4 us
  Pallas kernels  96 us (96%)
  between operations  3.45 us (3%)
    pallas_call x1, Pallas kernels, on_device_small(): pl.pallas_call(layer_kernel, out_shape=(*large, shape((16, 128), F32)), i...  92.8 us
    pallas_call x1, Pallas kernels, on_device_small(): pl.pallas_call(hand_on_kernel, out_shape=large + (shape((24,), F32),) * 8...  3.17 us

profile of v3, /device:TPU:0, one launch (start us, length us, event | category | flops | bytes accessed | tf_op | source)
XLA Modules:
  0.0 99.4 jit_solution(2447895366001123116)
XLA Ops:
  3.2 92.8 %encoder_layer.1 = (bf16[32,768]{1,0:T(8,128)(2,1)}, bf16[440,768]{1,0:T(8,128)(2,1)}, f32[32,768]{1,0:T(8,128)}, f32[440,768]{1,0:T(8,128)}, f32[24,768]{1,0:T(...) custom-call(bf16[32,768]{1,0:T(8,128)(2,1)} %qtok.1, ...), custom_call_target="tpu_custom_call" | custom-call | tf_op jit(solution)/shard_map/encoder_layer/pallas_call | solution.py:1304
  96.0 3.2 %hand_on.1 = (bf16[32,768]{1,0:T(8,128)(2,1)}, bf16[440,768]{1,0:T(8,128)(2,1)}, f32[32,768]{1,0:T(8,128)}, f32[440,768]{1,0:T(8,128)}, f32[24,768]{1,0:T(8,128)...) custom-call(bf16[32,768]{1,0:T(8,128)(2,1)} %get-tuple-element.51.re, ...), custom_call_target="tpu_custom_call" | custom-call | tf_op jit(solution)/shard_map/hand_on/pallas_call | solution.py:1357

commit v4 on v3

--- a/solution.py
+++ b/solution.py
@@ -788,7 +788,7 @@
     across.start()
     across.wait()
 
-    ex_f[...] = ex[...].astype(F32)
+    ex_f[0:1024, :] = ex[...].astype(F32)
 
     def first(r):
         return ex_f[pl.ds(r, 32, stride=32), :]
@@ -1199,8 +1199,8 @@
 
     def vec_part(whole, to):
         device = to * 8 + plane
-        narrow = pltpu.roll(whole[0:8], D - 24 * device, 1)[:, 0:128]
-        wide = pltpu.roll(whole[8:16], D - 96 * plane, 1)[:, 0:128]
+        narrow = pltpu.roll(whole[0:8], lax.rem(D - 24 * device, D), 1)[:, 0:128]
+        wide = pltpu.roll(whole[8:16], lax.rem(D - 96 * plane, D), 1)[:, 0:128]
         wide = jnp.sum(jnp.where(iota((8, 128), 0) == to, wide, 0.0), axis=0, keepdims=True)
         return jnp.concatenate([narrow, wide, jnp.zeros((7, 128), F32)], axis=0)
 
@@ -1326,7 +1326,7 @@
             pltpu.VMEM((256, D), F32), pltpu.VMEM((256, D), F32),
             pltpu.VMEM((ROWS, FF), BF16),
             pltpu.VMEM((32, D), BF16), pltpu.VMEM((440, D), BF16), pltpu.VMEM((32, D), BF16), pltpu.VMEM((440, D), BF16),
-            pltpu.VMEM((1024, 128), BF16), pltpu.VMEM((1024, 128), F32),
+            pltpu.VMEM((1024, 128), BF16), pltpu.VMEM((1056, 128), F32),
             pltpu.VMEM((16, D), F32), pltpu.VMEM((3, 16, D), F32), pltpu.VMEM((3, 16, 128), F32), pltpu.VMEM((3, 16, 128), F32),
             pltpu.VMEM((16, 128), F32), pltpu.VMEM((6, 3, 48, WIDE), F32),
             pltpu.VMEM((4, 3, 2, 4, 2, 2, 48, WIDE), BF16),

time: 99.7 us -> 99.6 us (level)
  no operation moved by 1% of the time
where the time goes in v4:
time: 99.6 us; the launch traced here: 99.4 us
  Pallas kernels  96 us (96%)
  between operations  3.45 us (3%)
    pallas_call x1, Pallas kernels, on_device_small(): pl.pallas_call(layer_kernel, out_shape=(*large, shape((16, 128), F32)), i...  92.8 us
    pallas_call x1, Pallas kernels, on_device_small(): pl.pallas_call(hand_on_kernel, out_shape=large + (shape((24,), F32),) * 8...  3.17 us

profile of v4, /device:TPU:0, one launch (start us, length us, event | category | flops | bytes accessed | tf_op | source)
XLA Modules:
  0.0 99.4 jit_solution(3658361674994078552)
XLA Ops:
  3.2 92.8 %encoder_layer.1 = (bf16[32,768]{1,0:T(8,128)(2,1)}, bf16[440,768]{1,0:T(8,128)(2,1)}, f32[32,768]{1,0:T(8,128)}, f32[440,768]{1,0:T(8,128)}, f32[24,768]{1,0:T(...) custom-call(bf16[32,768]{1,0:T(8,128)(2,1)} %qtok.1, ...), custom_call_target="tpu_custom_call" | custom-call | tf_op jit(solution)/shard_map/encoder_layer/pallas_call | solution.py:1304
  96.0 3.2 %hand_on.1 = (bf16[32,768]{1,0:T(8,128)(2,1)}, bf16[440,768]{1,0:T(8,128)(2,1)}, f32[32,768]{1,0:T(8,128)}, f32[440,768]{1,0:T(8,128)}, f32[24,768]{1,0:T(8,128)...) custom-call(bf16[32,768]{1,0:T(8,128)(2,1)} %get-tuple-element.51.re, ...), custom_call_target="tpu_custom_call" | custom-call | tf_op jit(solution)/shard_map/hand_on/pallas_call | solution.py:1357
